TPU v7x, 32 devices: a whole 2x2x4 slice. The times are simulated.
32 devices in a mesh: user: 2 (over x), item: 4 (over z), feat: 4 (over y, core).
Axes of the slice: x: 2, y: 2, z: 4, core: 2. Of those that a mesh axis runs over, the one named last changes fastest.
Arguments:
- tensor_tiles: bfloat16 [64, 256, 16384], P(('user', 'item', 'feat')), may hold values from -6 to 6
- tile_coords: int32 [64, 3], P(('user', 'item', 'feat')), may hold values from 0 to 7, as said below
- tile_live: int32 [64], P(('user', 'item', 'feat')), may hold values from 0 to 1, as said below
- side_matrix: bfloat16 [1024, 32768], P(('user', 'item'), 'feat'), may hold values from -6 to 6
- user_factor: bfloat16 [1024, 384], P('user'), may hold values from -2.1875 to 2.1875
- item_factor: bfloat16 [2048, 384], P('item'), may hold values from -2.1875 to 2.1875
- week_factor: bfloat16 [256, 384], replicated, may hold values from -2.1875 to 2.1875
- feat_factor: bfloat16 [384, 32768], P(('user', 'item'), 'feat'), may hold values from -0.59765625 to 0.59765625
Outputs:
- grad_user: float32 [1024, 384], P(('user', 'item', 'feat'))
- grad_item: float32 [2048, 384], P(None, ('user', 'item', 'feat'))
- grad_week: float32 [256, 384], P(None, ('user', 'item', 'feat'))
- grad_feat: float32 [384, 32768], P(('user', 'item'), 'feat')
Inputs may be any that keep to these rules, and one draw needn't show every extreme that they name: `tile_coords`: column 0 is a user block, column 1 an item block, column 2 a week block. A slot on the device with user index u and item index i has its user block in u * 2 to u * 2 + 1 and its item block in i * 2 to i * 2 + 1. `tile_live`: on every device the live slots come first. Two devices whose feat indices differ only in the lowest bit hold 2 live slots together.
All inputs are finite; a program needn't handle non-finite values.
Results may differ from a plain program's by a relative error of at most 0.0014.
Values may be sent and summed in bfloat16 or wider, within the bound.
A program may use at most 128 MiB of HBM per device.

v0:
```python
import jax
import jax.numpy as jnp
from jax import lax
from jax.sharding import PartitionSpec as P

BU = 256
BI = 256
BW = 64


tensor_scale = 0.015625
side_scale = 0.03125


def tile_terms(block_tile, user_block, item_block, week_block):
    rows_item = item_block.shape[0]
    rows_week = week_block.shape[0]
    rank_width = user_block.shape[1]
    khatri = (
        (item_block.astype(jnp.float32)[:, None, :] * week_block.astype(jnp.float32)[None, :, :])
        .reshape(rows_item * rows_week, rank_width)
        .astype(jnp.bfloat16)
    )
    predicted = lax.dot_general(
        user_block, khatri, (((1,), (1,)), ((), ())), preferred_element_type=jnp.float32
    )
    residual = (tensor_scale * (predicted - block_tile.astype(jnp.float32))).astype(jnp.bfloat16)
    user_term = jnp.dot(residual, khatri, preferred_element_type=jnp.float32)
    crossed = lax.dot_general(
        residual, user_block, (((0,), (0,)), ((), ())), preferred_element_type=jnp.float32
    ).reshape(rows_item, rows_week, rank_width)
    item_term = jnp.sum(crossed * week_block.astype(jnp.float32)[None, :, :], axis=1)
    week_term = jnp.sum(crossed * item_block.astype(jnp.float32)[:, None, :], axis=0)
    return (user_term, item_term, week_term)


def add_rows(buffer, first_row, addend):
    current = lax.dynamic_slice_in_dim(buffer, first_row, addend.shape[0], 0)
    return lax.dynamic_update_slice_in_dim(buffer, current + addend, first_row, 0)


def local(
    tensor_tiles,
    tile_coords,
    tile_live,
    side_matrix,
    user_factor,
    item_factor,
    week_factor,
    feat_factor,
):
    user_rows = user_factor.shape[0]
    item_rows = item_factor.shape[0]
    rank_width = user_factor.shape[1]
    user_base = lax.axis_index("user") * user_rows
    item_base = lax.axis_index("item") * item_rows
    item_total = item_rows * lax.axis_size("item")
    running = (
        jnp.zeros((user_rows, rank_width), jnp.float32),
        jnp.zeros((item_total, rank_width), jnp.float32),
        jnp.zeros((week_factor.shape[0], rank_width), jnp.float32),
    )

    def one_slot(slot_index, sums):
        user_sum, item_sum, week_sum = sums
        coords = lax.dynamic_index_in_dim(tile_coords, slot_index, 0, keepdims=False)
        user_start = coords[0] * BU - user_base
        item_start = coords[1] * BI
        week_start = coords[2] * BW

        def live_terms(unused):
            block_tile = lax.dynamic_index_in_dim(tensor_tiles, slot_index, 0, keepdims=False)
            user_block = lax.dynamic_slice_in_dim(user_factor, user_start, BU, 0)
            item_block = lax.dynamic_slice_in_dim(item_factor, item_start - item_base, BI, 0)
            week_block = lax.dynamic_slice_in_dim(week_factor, week_start, BW, 0)
            return tile_terms(block_tile, user_block, item_block, week_block)

        def dead_terms(unused):
            return (
                jnp.zeros((BU, rank_width), jnp.float32),
                jnp.zeros((BI, rank_width), jnp.float32),
                jnp.zeros((BW, rank_width), jnp.float32),
            )

        is_live = lax.dynamic_index_in_dim(tile_live, slot_index, 0, keepdims=False)
        user_term, item_term, week_term = lax.cond(is_live > 0, live_terms, dead_terms, 0)
        return (
            add_rows(user_sum, user_start, user_term),
            add_rows(item_sum, item_start, item_term),
            add_rows(week_sum, week_start, week_term),
        )

    running = lax.fori_loop(0, tensor_tiles.shape[0], one_slot, running)
    user_sum, item_sum, week_sum = running
    side_cols, factor_cols = (
        lax.all_to_all(side_matrix, ("user", "item"), split_axis=1, concat_axis=0, tiled=True),
        lax.all_to_all(feat_factor, ("user", "item"), split_axis=1, concat_axis=0, tiled=True),
    )
    all_users = lax.all_gather(user_factor, "user", axis=0, tiled=True)
    predicted = jnp.dot(all_users, factor_cols, preferred_element_type=jnp.float32)
    side_resid = (side_scale * (predicted - side_cols.astype(jnp.float32))).astype(jnp.bfloat16)
    side_user = lax.dot_general(
        side_resid, factor_cols, (((1,), (1,)), ((), ())), preferred_element_type=jnp.float32
    )
    feat_cols = lax.dot_general(
        all_users, side_resid, (((0,), (0,)), ((), ())), preferred_element_type=jnp.float32
    )
    grad_feat = lax.all_to_all(feat_cols, ("user", "item"), split_axis=0, concat_axis=1, tiled=True)
    user_total = add_rows(side_user, user_base, user_sum)
    grad_user = lax.psum_scatter(
        user_total, ("user", "item", "feat"), scatter_dimension=0, tiled=True
    )
    grad_item, grad_week = (
        lax.psum_scatter(item_sum, ("user", "item", "feat"), scatter_dimension=1, tiled=True),
        lax.psum_scatter(week_sum, ("user", "item", "feat"), scatter_dimension=1, tiled=True),
    )
    return (grad_user, grad_item, grad_week, grad_feat)


def solution(mesh):
    return jax.shard_map(
        local,
        mesh=mesh,
        in_specs=(
            P(("user", "item", "feat"), None, None),
            P(("user", "item", "feat"), None),
            P(("user", "item", "feat")),
            P(("user", "item"), "feat"),
            P("user", None),
            P("item", None),
            P(),
            P(("user", "item"), "feat"),
        ),
        out_specs=(
            P(("user", "item", "feat"), None),
            P(None, ("user", "item", "feat")),
            P(None, ("user", "item", "feat")),
            P(("user", "item"), "feat"),
        ),
        check_vma=False,
    )
```

profile of v0, /device:TPU:1, one launch (start us, length us, event | category | flops | bytes accessed | tf_op | source)
XLA Modules:
  0.0 379.0 jit_solution(16568169304780579496)
XLA Ops:
  7.2 2.2 copy.39
  9.4 6.4 %all-to-all-start = ((bf16[48,8,1024]{2,0,1:T(8,128)(2,1)}), bf16[48,8,1024]{2,0,1:T(8,128)(2,1)S(1)}, u32[]{:S(2)}, u32[]{:S(2)}) async-start(bf16[48,8,1024]{2,0,1:T(8,128)(2,1)} %bitcast.44), calls=%async_computation | async-start | bytes 1572864 | tf_op jit(solution)/shard_map/all_to_all | solution.py:97
  15.8 1.6 copy.38
  17.4 18.2 %all-to-all-done = bf16[48,8,1024]{2,0,1:T(8,128)(2,1)S(1)} async-done(((bf16[48,8,1024]{2,0,1:T(8,128)(2,1)}), bf16[48,8,1024]{2,0,1:T(8,128)(2,1)S(1)}, u32[]{:S(2)}, u32[]{:S(2)}) %all-to-all-start) | async-done | bytes 786464 | tf_op jit(solution)/shard_map/all_to_all | solution.py:97
  35.6 3.6 all-to-all-start.1
  39.2 19.9 %all_gather.3 = bf16[1024,384]{1,0:T(8,128)(2,1)} all-gather(bf16[512,384]{1,0:T(8,128)(2,1)S(1)} %copy-done.1), channel_id=1, replica_groups=mesh['user'=2,'item'=4,'feat'=4] {'user'}, dimensions={0}, use_global_device_ids=true | all-gather | bytes 1179648 | tf_op jit(solution)/shard_map/all_gather | solution.py:99
  59.1 27.0 %all-to-all-done.1 = bf16[128,8,1024]{2,0,1:T(8,128)(2,1)S(1)} async-done(((bf16[128,8,1024]{2,0,1:T(8,128)(2,1)}), bf16[128,8,1024]{2,0,1:T(8,128)(2,1)S(1)}, u32[]{:S(2)}, u32[]{:S(2)}) %all-to-all-start.1) | async-done | bytes 2097184 | tf_op jit(solution)/shard_map/all_to_all | solution.py:96
  86.1 2.5 fusion.10
  88.6 2.2 fusion.15
  90.7 4.4 %all-to-all-start.2 = ((f32[8,48,1024]{2,1,0:T(8,128)}), f32[8,48,1024]{2,1,0:T(8,128)}, u32[]{:S(2)}, u32[]{:S(2)}) async-start(f32[8,48,1024]{2,1,0:T(8,128)} %bitcast.12), calls=%async_computation.3 | async-start | bytes 3145728 | tf_op jit(solution)/shard_map/all_to_all | solution.py:108
  95.3 2.1 broadcast_in_dim.5.clone
  97.4 12.9 %while.17 = (s32[]{:T(128)}, f32[512,384]{1,0:T(8,128)S(1)}, f32[2048,384]{0,1:T(8,128)}, f32[256,384]{1,0:T(8,128)S(1)}, s32[2,3]{1,0:T(2,128)S(1)}, /*index=5*...) while((s32[]{:T(128)}, f32[512,384]{1,0:T(8,128)S(1)}, ...), condition=%wide.region_5.6_spmd, body=%wide.region_0.5_spmd.sunk | while | flops 9718423552 | bytes 163988208 | solution.py:93
  110.3 3.0 fusion.14
  114.9 189.4 %fusion.11 = (f32[2048,16]{0,1:T(8,128)S(1)}, f32[256,16]{0,1:T(8,128)S(1)}) fusion(f32[2048,384]{0,1:T(8,128)} %get-tuple-element.236, f32[256,384]{0,1:T(8,128)S(1)} %copy.28), kind=kCustom, calls=%all-reduce-scatter.2 | all-reduce-scatter fusion | flops 1179649 | bytes 3686400
  304.3 1.3 collective-permute-start.6
  305.6 3.5 collective-permute-start.5
  309.2 6.5 %collective-permute-start.7 = (f32[2048,12]{0,1:T(8,128)S(1)}, f32[2048,12]{0,1:T(8,128)S(1)}, u32[]{:S(2)}, u32[]{:S(2)}) collective-permute-start(f32[2048,12]{0,1:T(8,128)S(1)} %slice.24), channel_id=1, source_target_pairs={{0,8},{1,9},{2,10},{3,11},{4,12},{5,13},{6,14},{7,15},{8,16},{9,17... | collective-permute-start | bytes 294920
  315.7 2.2 collective-permute-start.14
  317.9 1.6 collective-permute-start.15
  320.4 5.5 %collective-permute-start.13 = (f32[256,16]{0,1:T(8,128)S(1)}, f32[256,16]{0,1:T(8,128)S(1)}, u32[]{:S(2)}, u32[]{:S(2)}) collective-permute-start(f32[256,16]{0,1:T(8,128)S(1)} %get-tuple-element.265), channel_id=1, source_target_pairs={{0,6},{1,7},{2,8},{3,9},{4,10},{5,11},{6,12},{7,13},{8,14},{9,15},... | collective-permute-start | bytes 49160
  326.0 2.1 collective-permute-start.12
  328.0 4.6 %collective-permute-start.11 = (f32[256,16]{0,1:T(8,128)S(1)}, f32[256,16]{0,1:T(8,128)S(1)}, u32[]{:S(2)}, u32[]{:S(2)}) collective-permute-start(f32[256,16]{0,1:T(8,128)S(1)} %get-tuple-element.265), channel_id=1, source_target_pairs={{0,4},{1,5},{2,6},{3,7},{4,8},{5,9},{6,10},{7,11},{8,12},{9,13},{1... | collective-permute-start | bytes 49160
  332.7 6.9 %collective-permute-start.10 = (f32[256,16]{0,1:T(8,128)S(1)}, f32[256,16]{0,1:T(8,128)S(1)}, u32[]{:S(2)}, u32[]{:S(2)}) collective-permute-start(f32[256,16]{0,1:T(8,128)S(1)} %get-tuple-element.265), channel_id=1, source_target_pairs={{0,3},{1,4},{2,5},{3,6},{4,7},{5,8},{6,9},{7,10},{8,11},{9,12},{10... | collective-permute-start | bytes 49160
  339.6 3.4 collective-permute-start.9
  342.9 3.7 collective-permute-start.8
  346.6 3.6 collective-permute-start.4
  350.2 3.3 collective-permute-start.3
  353.6 3.5 collective-permute-start.2
  357.1 6.4 %collective-permute-start.1 = (f32[2048,16]{0,1:T(8,128)S(1)}, f32[2048,16]{0,1:T(8,128)S(1)}, u32[]{:S(2)}, u32[]{:S(2)}) collective-permute-start(f32[2048,16]{0,1:T(8,128)S(1)} %get-tuple-element.264), channel_id=1, source_target_pairs={{0,2},{1,3},{2,4},{3,5},{4,6},{5,7},{6,8},{7,9},{8,10},{9,11},{10,... | collective-permute-start | bytes 393224
  363.5 1.9 collective-permute-start
  367.4 1.4 concatenate
  369.5 2.7 copy.35
  (73 shorter events, 12.8 us)
Async XLA Ops:
  7.2 8.6 %copy-start.3 = (bf16[128,8192]{1,0:T(8,128)(2,1)S(1)}, bf16[128,8192]{1,0:T(8,128)(2,1)}, u32[]{:S(2)}) copy-start(bf16[128,8192]{1,0:T(8,128)(2,1)} %param.15) | copy-start | bytes 6291460
  9.4 26.2 %all-to-all-start = ((bf16[48,8,1024]{2,0,1:T(8,128)(2,1)}), bf16[48,8,1024]{2,0,1:T(8,128)(2,1)S(1)}, u32[]{:S(2)}, u32[]{:S(2)}) async-start(bf16[48,8,1024]{2,0,1:T(8,128)(2,1)} %bitcast.44), calls=%async_computation | async-start | bytes 1572864 | tf_op jit(solution)/shard_map/all_to_all | solution.py:97
  15.8 23.4 %copy-start.1 = (bf16[512,384]{1,0:T(8,128)(2,1)S(1)}, bf16[512,384]{1,0:T(8,128)(2,1)}, u32[]{:S(2)}) copy-start(bf16[512,384]{1,0:T(8,128)(2,1)} %param.16) | copy-start | bytes 1179652
  35.6 53.0 %copy-start.4 = (bf16[48,8,1024]{2,0,1:T(8,128)(2,1)}, bf16[48,8,1024]{2,0,1:T(8,128)(2,1)S(1)}, u32[]{:S(2)}) copy-start(bf16[48,8,1024]{2,0,1:T(8,128)(2,1)S(1)} %all-to-all-done) | copy-start | bytes 2359300
  35.6 50.5 %all-to-all-start.1 = ((bf16[128,8,1024]{2,0,1:T(8,128)(2,1)}), bf16[128,8,1024]{2,0,1:T(8,128)(2,1)S(1)}, u32[]{:S(2)}, u32[]{:S(2)}) async-start(bf16[128,8,1024]{2,0,1:T(8,128)(2,1)} %bitcast.43), calls=%async_computation.1 | async-start | bytes 4194304 | tf_op jit(solution)/shard_map/all_to_all | solution.py:96
  86.1 2.5 copy-start.5
  88.5 2.2 copy-start.8
  90.7 6.7 %copy-start.6 = (s32[2,3]{1,0:T(2,128)S(1)}, s32[2,3]{1,0:T(2,128)}, u32[]{:S(2)}) copy-start(s32[2,3]{1,0:T(2,128)} %param.13) | copy-start | bytes 76
  90.7 6.7 %copy-start.7 = (s32[2]{0:T(128)S(1)}, s32[2]{0:T(128)}, u32[]{:S(2)}) copy-start(s32[2]{0:T(128)} %param.14) | copy-start | bytes 28
  90.7 278.7 %all-to-all-start.2 = ((f32[8,48,1024]{2,1,0:T(8,128)}), f32[8,48,1024]{2,1,0:T(8,128)}, u32[]{:S(2)}, u32[]{:S(2)}) async-start(f32[8,48,1024]{2,1,0:T(8,128)} %bitcast.12), calls=%async_computation.3 | async-start | bytes 3145728 | tf_op jit(solution)/shard_map/all_to_all | solution.py:108
  95.2 277.0 %reduce-scatter.6.cloned.1.call-start = ((), (), s32[]{:S(2)}) async-start(), calls=%async_computation.4 | async-start | bytes 1622016 | tf_op jit(solution)/shard_map/reduce_scatter | solution.py:110
  113.5 1.2 copy-start.2
  304.3 52.8 %collective-permute-start.6 = (f32[2048,16]{0,1:T(8,128)S(1)}, f32[2048,16]{0,1:T(8,128)S(1)}, u32[]{:S(2)}, u32[]{:S(2)}) collective-permute-start(f32[2048,16]{0,1:T(8,128)S(1)} %get-tuple-element.264), channel_id=1, source_target_pairs={{0,7},{1,8},{2,9},{3,10},{4,11},{5,12},{6,13},{7,14},{8,15},{9,16}... | collective-permute-start | bytes 393224
  305.6 57.9 %collective-permute-start.5 = (f32[2048,16]{0,1:T(8,128)S(1)}, f32[2048,16]{0,1:T(8,128)S(1)}, u32[]{:S(2)}, u32[]{:S(2)}) collective-permute-start(f32[2048,16]{0,1:T(8,128)S(1)} %get-tuple-element.264), channel_id=1, source_target_pairs={{0,6},{1,7},{2,8},{3,9},{4,10},{5,11},{6,12},{7,13},{8,14},{9,15},... | collective-permute-start | bytes 393224
  309.2 44.4 %collective-permute-start.7 = (f32[2048,12]{0,1:T(8,128)S(1)}, f32[2048,12]{0,1:T(8,128)S(1)}, u32[]{:S(2)}, u32[]{:S(2)}) collective-permute-start(f32[2048,12]{0,1:T(8,128)S(1)} %slice.24), channel_id=1, source_target_pairs={{0,8},{1,9},{2,10},{3,11},{4,12},{5,13},{6,14},{7,15},{8,16},{9,17... | collective-permute-start | bytes 294920
  315.7 10.3 %collective-permute-start.14 = (f32[256,16]{0,1:T(8,128)S(1)}, f32[256,16]{0,1:T(8,128)S(1)}, u32[]{:S(2)}, u32[]{:S(2)}) collective-permute-start(f32[256,16]{0,1:T(8,128)S(1)} %get-tuple-element.265), channel_id=1, source_target_pairs={{0,7},{1,8},{2,9},{3,10},{4,11},{5,12},{6,13},{7,14},{8,15},{9,16}... | collective-permute-start | bytes 49160
  317.9 2.5 collective-permute-start.15
  320.4 7.6 %collective-permute-start.13 = (f32[256,16]{0,1:T(8,128)S(1)}, f32[256,16]{0,1:T(8,128)S(1)}, u32[]{:S(2)}, u32[]{:S(2)}) collective-permute-start(f32[256,16]{0,1:T(8,128)S(1)} %get-tuple-element.265), channel_id=1, source_target_pairs={{0,6},{1,7},{2,8},{3,9},{4,10},{5,11},{6,12},{7,13},{8,14},{9,15},... | collective-permute-start | bytes 49160
  326.0 6.7 %collective-permute-start.12 = (f32[256,16]{0,1:T(8,128)S(1)}, f32[256,16]{0,1:T(8,128)S(1)}, u32[]{:S(2)}, u32[]{:S(2)}) collective-permute-start(f32[256,16]{0,1:T(8,128)S(1)} %get-tuple-element.265), channel_id=1, source_target_pairs={{0,5},{1,6},{2,7},{3,8},{4,9},{5,10},{6,11},{7,12},{8,13},{9,14},{... | collective-permute-start | bytes 49160
  328.0 11.5 %collective-permute-start.11 = (f32[256,16]{0,1:T(8,128)S(1)}, f32[256,16]{0,1:T(8,128)S(1)}, u32[]{:S(2)}, u32[]{:S(2)}) collective-permute-start(f32[256,16]{0,1:T(8,128)S(1)} %get-tuple-element.265), channel_id=1, source_target_pairs={{0,4},{1,5},{2,6},{3,7},{4,8},{5,9},{6,10},{7,11},{8,12},{9,13},{1... | collective-permute-start | bytes 49160
  332.7 10.2 %collective-permute-start.10 = (f32[256,16]{0,1:T(8,128)S(1)}, f32[256,16]{0,1:T(8,128)S(1)}, u32[]{:S(2)}, u32[]{:S(2)}) collective-permute-start(f32[256,16]{0,1:T(8,128)S(1)} %get-tuple-element.265), channel_id=1, source_target_pairs={{0,3},{1,4},{2,5},{3,6},{4,7},{5,8},{6,9},{7,10},{8,11},{9,12},{10... | collective-permute-start | bytes 49160
  339.6 7.0 %collective-permute-start.9 = (f32[256,16]{0,1:T(8,128)S(1)}, f32[256,16]{0,1:T(8,128)S(1)}, u32[]{:S(2)}, u32[]{:S(2)}) collective-permute-start(f32[256,16]{0,1:T(8,128)S(1)} %get-tuple-element.265), channel_id=1, source_target_pairs={{0,2},{1,3},{2,4},{3,5},{4,6},{5,7},{6,8},{7,9},{8,10},{9,11},{10,... | collective-permute-start | bytes 49160
  342.9 7.3 %collective-permute-start.8 = (f32[256,16]{0,1:T(8,128)S(1)}, f32[256,16]{0,1:T(8,128)S(1)}, u32[]{:S(2)}, u32[]{:S(2)}) collective-permute-start(f32[256,16]{0,1:T(8,128)S(1)} %get-tuple-element.265), channel_id=1, source_target_pairs={{0,1},{1,2},{2,3},{3,4},{4,5},{5,6},{6,7},{7,8},{8,9},{9,10},{10,1... | collective-permute-start | bytes 49160
  346.6 20.4 %collective-permute-start.4 = (f32[2048,16]{0,1:T(8,128)S(1)}, f32[2048,16]{0,1:T(8,128)S(1)}, u32[]{:S(2)}, u32[]{:S(2)}) collective-permute-start(f32[2048,16]{0,1:T(8,128)S(1)} %get-tuple-element.264), channel_id=1, source_target_pairs={{0,5},{1,6},{2,7},{3,8},{4,9},{5,10},{6,11},{7,12},{8,13},{9,14},{... | collective-permute-start | bytes 393224
  350.2 16.8 %collective-permute-start.3 = (f32[2048,16]{0,1:T(8,128)S(1)}, f32[2048,16]{0,1:T(8,128)S(1)}, u32[]{:S(2)}, u32[]{:S(2)}) collective-permute-start(f32[2048,16]{0,1:T(8,128)S(1)} %get-tuple-element.264), channel_id=1, source_target_pairs={{0,4},{1,5},{2,6},{3,7},{4,8},{5,9},{6,10},{7,11},{8,12},{9,13},{1... | collective-permute-start | bytes 393224
  353.6 13.4 %collective-permute-start.2 = (f32[2048,16]{0,1:T(8,128)S(1)}, f32[2048,16]{0,1:T(8,128)S(1)}, u32[]{:S(2)}, u32[]{:S(2)}) collective-permute-start(f32[2048,16]{0,1:T(8,128)S(1)} %get-tuple-element.264), channel_id=1, source_target_pairs={{0,3},{1,4},{2,5},{3,6},{4,7},{5,8},{6,9},{7,10},{8,11},{9,12},{10... | collective-permute-start | bytes 393224
  357.1 9.9 %collective-permute-start.1 = (f32[2048,16]{0,1:T(8,128)S(1)}, f32[2048,16]{0,1:T(8,128)S(1)}, u32[]{:S(2)}, u32[]{:S(2)}) collective-permute-start(f32[2048,16]{0,1:T(8,128)S(1)} %get-tuple-element.264), channel_id=1, source_target_pairs={{0,2},{1,3},{2,4},{3,5},{4,6},{5,7},{6,8},{7,9},{8,10},{9,11},{10,... | collective-permute-start | bytes 393224
  363.5 3.9 %collective-permute-start = (f32[2048,16]{0,1:T(8,128)S(1)}, f32[2048,16]{0,1:T(8,128)S(1)}, u32[]{:S(2)}, u32[]{:S(2)}) collective-permute-start(f32[2048,16]{0,1:T(8,128)S(1)} %get-tuple-element.264), channel_id=1, source_target_pairs={{0,1},{1,2},{2,3},{3,4},{4,5},{5,6},{6,7},{7,8},{8,9},{9,10},{10,1... | collective-permute-start | bytes 393224
Sparse Core Ops, SparseCore 0:
  114.9 213.0 reduce-scatter.5
where the time goes:
time: 384 us; the launch traced here: 379 us
  blocking collectives  209 us (54%)
  starting transfers between devices  74.5 us (19%)
  waiting for transfers between devices  46.4 us (12%)
  local copies, waits for them, and re-layouts  20.9 us (5%)
  between operations  14.4 us (4%)
  matrix products  7.66 us (2%)
  loops' own time  5.5 us (1%)
    unnamed x1, blocking collectives  189 us
    unnamed x16, starting transfers between devices  60 us
    all_to_all x1, waiting for transfers between devices, local(): lax.all_to_all(side_matrix, ('user', 'item'), split_axis=1, concat_axis=0...  27 us
    all_gather x1, blocking collectives, local(): all_users = lax.all_gather(user_factor, 'user', axis=0, tiled=True)  19.9 us
    all_to_all x1, waiting for transfers between devices, local(): lax.all_to_all(feat_factor, ('user', 'item'), split_axis=1, concat_axis=0...  18.2 us
  transfers between devices with their start and end apart: 20, of which 4 were waited for; matrix products, arithmetic and copies ran while one was open for 55% of the time, Pallas kernels for 0%

commit v1 on v0

v1 whole, which is shorter than its diff:
```python
import jax
import jax.numpy as jnp
from jax import lax
from jax.experimental import pallas as pl
from jax.experimental.pallas import tpu as pltpu
from jax.sharding import PartitionSpec as P

BU = 256
BI = 256
BW = 64
ITEMS_STEP = 16

tensor_scale = 0.015625
side_scale = 0.03125


def tile_kernel(starts, live, tile, user, item, week, user_sum, item_sum, week_sum):
    slot = pl.program_id(0)
    step = pl.program_id(1)

    @pl.when((slot == 0) & (step == 0))
    def _():
        user_sum[...] = jnp.zeros_like(user_sum)
        item_sum[...] = jnp.zeros_like(item_sum)
        week_sum[...] = jnp.zeros_like(week_sum)

    @pl.when(live[slot] > 0)
    def _():
        user_rows = pl.ds(pl.multiple_of(starts[slot, 0], BU), BU)
        item_rows = pl.ds(
            pl.multiple_of(starts[slot, 1] + step * ITEMS_STEP, ITEMS_STEP), ITEMS_STEP
        )
        week_rows = pl.ds(pl.multiple_of(starts[slot, 2], BW), BW)
        users = user[user_rows, :]
        items = item[item_rows, :].astype(jnp.float32)
        weeks = week[week_rows, :].astype(jnp.float32)
        rank = users.shape[1]
        khatri = (
            (items[:, None, :] * weeks[None, :, :])
            .reshape(ITEMS_STEP * BW, rank)
            .astype(jnp.bfloat16)
        )
        predicted = lax.dot_general(
            users, khatri, (((1,), (1,)), ((), ())), preferred_element_type=jnp.float32
        )
        residual = (tensor_scale * (predicted - tile[0].astype(jnp.float32))).astype(
            jnp.bfloat16
        )
        user_sum[user_rows, :] += jnp.dot(residual, khatri, preferred_element_type=jnp.float32)
        crossed = lax.dot_general(
            residual, users, (((0,), (0,)), ((), ())), preferred_element_type=jnp.float32
        ).reshape(ITEMS_STEP, BW, rank)
        item_sum[item_rows, :] += jnp.sum(crossed * weeks[None, :, :], axis=1)
        week_sum[week_rows, :] += jnp.sum(crossed * items[:, None, :], axis=0)


def tile_sums(tensor_tiles, tile_coords, tile_live, user_factor, item_factor, week_factor):
    slots, _, width = tensor_tiles.shape
    rank = user_factor.shape[1]
    steps = BI // ITEMS_STEP
    starts = jnp.stack(
        [
            lax.rem(tile_coords[:, 0] * BU, user_factor.shape[0]),
            lax.rem(tile_coords[:, 1] * BI, item_factor.shape[0]),
            tile_coords[:, 2] * BW,
        ],
        axis=1,
    )

    def tile_map(s, j, starts, live):
        count = live[0]
        for k in range(1, slots):
            count += live[k]
        dead = s >= count
        return (
            jnp.where(dead, jnp.maximum(count - 1, 0), s),
            0,
            jnp.where(dead, jnp.where(count > 0, steps - 1, 0), j),
        )

    whole = lambda a: pl.BlockSpec(a.shape, lambda s, j, *_: (0, 0))
    outs = [
        jax.ShapeDtypeStruct(a.shape, jnp.float32)
        for a in (user_factor, item_factor, week_factor)
    ]
    return pl.pallas_call(
        tile_kernel,
        grid_spec=pltpu.PrefetchScalarGridSpec(
            num_scalar_prefetch=2,
            grid=(slots, steps),
            in_specs=[
                pl.BlockSpec((1, BU, ITEMS_STEP * BW), tile_map),
                whole(user_factor),
                whole(item_factor),
                whole(week_factor),
            ],
            out_specs=[whole(a) for a in outs],
        ),
        out_shape=outs,
        compiler_params=pltpu.CompilerParams(
            dimension_semantics=("arbitrary", "arbitrary"),
            vmem_limit_bytes=40 * 1024 * 1024,
        ),
        cost_estimate=pl.CostEstimate(
            flops=slots * 6 * BU * width * rank,
            bytes_accessed=slots * 2 * BU * width,
            transcendentals=0,
        ),
        name="tile_sums",
    )(starts, tile_live, tensor_tiles, user_factor, item_factor, week_factor)


def gather_rows(block, axis):
    count = lax.axis_size(axis)
    me = lax.axis_index(axis)
    rows = block.shape[0]
    whole = jnp.zeros((count * rows,) + block.shape[1:], block.dtype)
    for shift in range(count):
        piece = block
        if shift:
            piece = lax.ppermute(
                block, axis, [(k, (k + shift) % count) for k in range(count)]
            )
        whole = lax.dynamic_update_slice_in_dim(
            whole, piece, lax.rem(me - shift + count, count) * rows, 0
        )
    return whole


def exchange(blocks, axes):
    return lax.all_to_all(blocks, axes, split_axis=0, concat_axis=0, tiled=True)


def local(
    tensor_tiles,
    tile_coords,
    tile_live,
    side_matrix,
    user_factor,
    item_factor,
    week_factor,
    feat_factor,
):
    user_rows, rank = user_factor.shape
    item_rows = item_factor.shape[0]
    week_rows = week_factor.shape[0]
    n_user = lax.axis_size("user")
    n_item = lax.axis_size("item")
    n_feat = lax.axis_size("feat")
    own = rank // (n_user * n_item * n_feat)
    user_base = lax.axis_index("user") * user_rows

    factor_cols = lax.all_to_all(
        feat_factor, ("user", "item"), split_axis=1, concat_axis=0, tiled=True
    )
    side_cols = lax.all_to_all(
        side_matrix, ("user", "item"), split_axis=1, concat_axis=0, tiled=True
    )
    all_users = gather_rows(user_factor, "user")

    user_sum, item_sum, week_sum = tile_sums(
        tensor_tiles, tile_coords, tile_live, user_factor, item_factor, week_factor
    )

    both = jnp.concatenate([item_sum, week_sum], axis=0).T
    both = both.reshape(n_user, n_item, n_feat, own, item_rows + week_rows)
    both = both.transpose(0, 2, 1, 3, 4).reshape(
        n_user * n_feat, n_item * own, item_rows + week_rows
    )
    both = jnp.sum(exchange(both, ("user", "feat")), axis=0)
    both = exchange(both.reshape(n_item, own, item_rows + week_rows), "item")
    grad_item = both[:, :, :item_rows].transpose(0, 2, 1).reshape(n_item * item_rows, own)
    grad_week = jnp.sum(both[:, :, item_rows:], axis=0).T

    predicted = jnp.dot(all_users, factor_cols, preferred_element_type=jnp.float32)
    side_resid = (side_scale * (predicted - side_cols.astype(jnp.float32))).astype(jnp.bfloat16)
    feat_cols = lax.dot_general(
        all_users, side_resid, (((0,), (0,)), ((), ())), preferred_element_type=jnp.float32
    )
    grad_feat = lax.all_to_all(feat_cols, ("user", "item"), split_axis=0, concat_axis=1, tiled=True)
    side_user = lax.dot_general(
        side_resid, factor_cols, (((1,), (1,)), ((), ())), preferred_element_type=jnp.float32
    )
    mine = lax.dynamic_slice_in_dim(side_user, user_base, user_rows, 0)
    user_total = lax.dynamic_update_slice_in_dim(side_user, mine + user_sum, user_base, 0)
    rows = user_total.shape[0] // (n_user * n_item * n_feat)
    by_feat = user_total.reshape(n_user * n_item, n_feat, rows, rank).transpose(1, 0, 2, 3)
    by_feat = jnp.sum(exchange(by_feat, "feat"), axis=0)
    grad_user = jnp.sum(exchange(by_feat, ("user", "item")), axis=0)
    return (grad_user, grad_item, grad_week, grad_feat)


def solution(mesh):
    return jax.shard_map(
        local,
        mesh=mesh,
        in_specs=(
            P(("user", "item", "feat"), None, None),
            P(("user", "item", "feat"), None),
            P(("user", "item", "feat")),
            P(("user", "item"), "feat"),
            P("user", None),
            P("item", None),
            P(),
            P(("user", "item"), "feat"),
        ),
        out_specs=(
            P(("user", "item", "feat"), None),
            P(None, ("user", "item", "feat")),
            P(None, ("user", "item", "feat")),
            P(("user", "item"), "feat"),
        ),
        check_vma=False,
    )
```

time: 384 us -> 197 us (0.51)
  the two profiles are of different devices: /device:TPU:1 before, /device:TPU:0 now
where the time goes in v1:
time: 197 us; the launch traced here: 195 us
  waiting for transfers between devices  98 us (50%)
  Pallas kernels  36.2 us (18%)
  starting transfers between devices  31.3 us (16%)
  local copies, waits for them, and re-layouts  17.4 us (9%)
  matrix products  8.15 us (4%)
  other arithmetic  3.2 us (2%)
    all_to_all x4, waiting for transfers between devices, exchange(): return lax.all_to_all(blocks, axes, split_axis=0, concat_axis=0, tiled=True)  41.5 us
    pallas_call x1, Pallas kernels, tile_sums(): pl.pallas_call(tile_kernel, grid_spec=pltpu.PrefetchScalarGridSpec(num_sc...  36.2 us
    all_to_all x1, waiting for transfers between devices, local(): lax.all_to_all(feat_cols, ('user', 'item'), split_axis=0, concat_axis=1,...  34.3 us
    all_to_all x1, waiting for transfers between devices, local(): lax.all_to_all(feat_factor, ('user', 'item'), split_axis=1, concat_axis=0...  19.4 us
    all_to_all x4, starting transfers between devices, exchange(): return lax.all_to_all(blocks, axes, split_axis=0, concat_axis=0, tiled=True)  14.1 us
    all_to_all x1, starting transfers between devices, local(): lax.all_to_all(feat_factor, ('user', 'item'), split_axis=1, concat_axis=0...  7.25 us
    all_to_all x1, starting transfers between devices, local(): lax.all_to_all(side_matrix, ('user', 'item'), split_axis=1, concat_axis=0...  4.49 us
  transfers between devices with their start and end apart: 8, of which 7 were waited for; matrix products, arithmetic and copies ran while one was open for 12% of the time, Pallas kernels for 19%

profile of v1, /device:TPU:0, one launch (start us, length us, event | category | flops | bytes accessed | tf_op | source)
XLA Modules:
  0.0 195.1 jit_solution(13977458032106388626)
XLA Ops:
  0.6 2.2 %copy.52 = bf16[6,8,8,1024]{3,2,0,1:T(8,128)(2,1)} copy(bf16[6,8,8,1024]{3,2,1,0:T(8,128)(2,1)} %bitcast.52) | data formatting | bytes 1572864 | tf_op jit(solution)/shard_map/all_to_all | solution.py:153
  2.9 7.3 %all-to-all-start = ((bf16[48,8,1024]{2,0,1:T(8,128)(2,1)}), bf16[48,8,1024]{2,0,1:T(8,128)(2,1)S(1)}, u32[]{:S(2)}, u32[]{:S(2)}) async-start(bf16[48,8,1024]{2,0,1:T(8,128)(2,1)} %bitcast.44), calls=%async_computation | async-start | bytes 1572864 | tf_op jit(solution)/shard_map/all_to_all | solution.py:153
  10.1 1.6 copy.50
  11.7 19.4 %all-to-all-done = bf16[48,8,1024]{2,0,1:T(8,128)(2,1)S(1)} async-done(((bf16[48,8,1024]{2,0,1:T(8,128)(2,1)}), bf16[48,8,1024]{2,0,1:T(8,128)(2,1)S(1)}, u32[]{:S(2)}, u32[]{:S(2)}) %all-to-all-start) | async-done | bytes 786464 | tf_op jit(solution)/shard_map/all_to_all | solution.py:153
  31.1 0.9 copy-done.6
  32.0 4.5 %all-to-all-start.1 = ((bf16[128,8,1024]{2,0,1:T(8,128)(2,1)}), bf16[128,8,1024]{2,0,1:T(8,128)(2,1)}, u32[]{:S(2)}, u32[]{:S(2)}) async-start(bf16[128,8,1024]{2,0,1:T(8,128)(2,1)} %bitcast.46), calls=%async_computation.1 | async-start | bytes 4194304 | tf_op jit(solution)/shard_map/all_to_all | solution.py:156
  36.5 1.9 collective-permute-start
  38.6 36.2 %tile_sums.1 = (f32[512,384]{1,0:T(8,128)S(1)}, f32[512,384]{1,0:T(8,128)S(1)}, f32[256,384]{1,0:T(8,128)S(1)}) custom-call(s32[2,3]{1,0:T(2,128)S(1)} %pad_add_fusion.starts, s32[2]{0:T(128)S(1)} %copy-done.3, bf16[2,256,16384]{2,1,0:T(8,128)(2,1)} %tile.1, bf16[512,384]{1,0:T(8,128)(2,1)S(1)} %copy-done, bf16[512,384]{1,0:T(8,128)(2,1)S(1)} %copy-done.1, ...), custom_call_target="tpu_custom_call" | custom-call | flops 19327352832 | bytes 16777216 | tf_op jit(solution)/shard_map/tile_sums/pallas_call | solution.py:86
  75.0 1.4 copy.35
  76.3 1.4 reshape.35
  77.7 1.3 copy.40
  79.0 2.4 %reshape.40 = f32[8,48,768]{2,1,0:T(8,128)} reshape(f32[2,4,4,12,768]{4,3,2,1,0:T(8,128)} %copy.40) | data formatting | bytes 2359296 | tf_op jit(solution)/shard_map/reshape | solution.py:167
  81.6 2.8 %all-to-all-done.1 = bf16[128,8,1024]{2,0,1:T(8,128)(2,1)} async-done(((bf16[128,8,1024]{2,0,1:T(8,128)(2,1)}), bf16[128,8,1024]{2,0,1:T(8,128)(2,1)}, u32[]{:S(2)}, u32[]{:S(2)}) %all-to-all-start.1) | async-done | bytes 2097184 | tf_op jit(solution)/shard_map/all_to_all | solution.py:156
  84.4 3.6 %all-to-all-start.4 = ((f32[8,48,768]{2,1,0:T(8,128)}), f32[8,48,768]{2,1,0:T(8,128)S(1)}, u32[]{:S(2)}, u32[]{:S(2)}) async-start(f32[8,48,768]{2,1,0:T(8,128)} %reshape.40), calls=%async_computation.4 | async-start | bytes 2359296 | tf_op jit(solution)/shard_map/all_to_all | solution.py:131
  88.0 1.1 constant_dynamic-update-slice_fusion
  89.1 3.1 %fusion.1 = bf16[1024,1024]{1,0:T(8,128)(2,1)S(1)} fusion(bf16[1024,384]{1,0:T(8,128)(2,1)S(1)} %constant_dynamic-update-slice_fusion, bf16[384,1024]{1,0:T(8,128)(2,1)} %bitcast.53, bf16[128,8,1024]{2,0,1:T(8,128)(2,1)} %all-to-all-done.1), kind=kOutput, calls=%fused_computation.2 | convolution fusion | flops 809500672 | bytes 5767168 | tf_op jit(solution)/shard_map/dot_general | solution.py:175
  92.3 1.3 fusion.4
  93.7 1.3 copy.51
  95.0 8.8 %all-to-all-done.4 = f32[8,48,768]{2,1,0:T(8,128)S(1)} async-done(((f32[8,48,768]{2,1,0:T(8,128)}), f32[8,48,768]{2,1,0:T(8,128)S(1)}, u32[]{:S(2)}, u32[]{:S(2)}) %all-to-all-start.4) | async-done | bytes 1179680 | tf_op jit(solution)/shard_map/all_to_all | solution.py:131
  103.8 3.6 %all-to-all-start.2 = ((f32[4,8,32,384]{3,2,1,0:T(8,128)}), f32[4,8,32,384]{3,2,1,0:T(8,128)S(1)}, u32[]{:S(2)}, u32[]{:S(2)}) async-start(f32[4,8,32,384]{3,2,1,0:T(8,128)} %bitcast.43), calls=%async_computation.2 | async-start | bytes 3145728 | tf_op jit(solution)/shard_map/all_to_all | solution.py:131
  107.4 0.7 reduce_sum.38
  108.1 1.6 reshape.37
  109.7 17.7 %all-to-all-done.2 = f32[4,8,32,384]{3,2,1,0:T(8,128)S(1)} async-done(((f32[4,8,32,384]{3,2,1,0:T(8,128)}), f32[4,8,32,384]{3,2,1,0:T(8,128)S(1)}, u32[]{:S(2)}, u32[]{:S(2)}) %all-to-all-start.2) | async-done | bytes 1572896 | tf_op jit(solution)/shard_map/all_to_all | solution.py:131
  127.4 3.4 %all-to-all-start.5 = ((f32[4,12,768]{2,1,0:T(8,128)}), f32[4,12,768]{2,1,0:T(8,128)S(1)}, u32[]{:S(2)}, u32[]{:S(2)}) async-start(f32[4,12,768]{2,1,0:T(8,128)} %reshape.37), calls=%async_computation.5 | async-start | bytes 393216 | tf_op jit(solution)/shard_map/all_to_all | solution.py:131
  130.8 0.9 reduce_sum.36
  131.7 6.7 %all-to-all-done.5 = f32[4,12,768]{2,1,0:T(8,128)S(1)} async-done(((f32[4,12,768]{2,1,0:T(8,128)}), f32[4,12,768]{2,1,0:T(8,128)S(1)}, u32[]{:S(2)}, u32[]{:S(2)}) %all-to-all-start.5) | async-done | bytes 147488 | tf_op jit(solution)/shard_map/all_to_all | solution.py:131
  138.3 3.6 %all-to-all-start.3 = ((f32[8,32,384]{2,1,0:T(8,128)}), f32[8,32,384]{2,1,0:T(8,128)S(1)}, u32[]{:S(2)}, u32[]{:S(2)}) async-start(f32[8,32,384]{2,1,0:T(8,128)} %reduce_sum.36), calls=%async_computation.3 | async-start | bytes 786432 | tf_op jit(solution)/shard_map/all_to_all | solution.py:131
  141.9 3.7 %fusion.5 = f32[384,1024]{1,0:T(8,128)} fusion(bf16[1024,384]{1,0:T(8,128)(2,1)S(1)} %constant_dynamic-update-slice_fusion, bf16[1024,1024]{1,0:T(8,128)(2,1)} %copy-done.5), kind=kOutput, calls=%fused_computation.22 | convolution fusion | flops 805306368 | bytes 4456448 | tf_op jit(solution)/shard_map/dot_general | solution.py:177
  145.7 8.3 %all-to-all-done.3 = f32[8,32,384]{2,1,0:T(8,128)S(1)} async-done(((f32[8,32,384]{2,1,0:T(8,128)}), f32[8,32,384]{2,1,0:T(8,128)S(1)}, u32[]{:S(2)}, u32[]{:S(2)}) %all-to-all-start.3) | async-done | bytes 393248 | tf_op jit(solution)/shard_map/all_to_all | solution.py:131
  153.9 3.6 %all-to-all-start.6 = ((f32[8,48,1024]{2,1,0:T(8,128)}), f32[8,48,1024]{2,1,0:T(8,128)S(1)}, u32[]{:S(2)}, u32[]{:S(2)}) async-start(f32[8,48,1024]{2,1,0:T(8,128)} %bitcast.10), calls=%async_computation.6 | async-start | bytes 3145728 | tf_op jit(solution)/shard_map/all_to_all | solution.py:180
  159.6 34.3 %all-to-all-done.6 = f32[8,48,1024]{2,1,0:T(8,128)S(1)} async-done(((f32[8,48,1024]{2,1,0:T(8,128)}), f32[8,48,1024]{2,1,0:T(8,128)S(1)}, u32[]{:S(2)}, u32[]{:S(2)}) %all-to-all-start.6) | async-done | bytes 1572896 | tf_op jit(solution)/shard_map/all_to_all | solution.py:180
  193.9 1.2 copy.44
  (30 shorter events, 2.6 us)
Async XLA Ops:
  0.6 9.5 %copy-start.4 = (bf16[128,8192]{1,0:T(8,128)(2,1)S(1)}, bf16[128,8192]{1,0:T(8,128)(2,1)}, u32[]{:S(2)}) copy-start(bf16[128,8192]{1,0:T(8,128)(2,1)} %param.11) | copy-start | bytes 6291460
  2.9 28.3 %all-to-all-start = ((bf16[48,8,1024]{2,0,1:T(8,128)(2,1)}), bf16[48,8,1024]{2,0,1:T(8,128)(2,1)S(1)}, u32[]{:S(2)}, u32[]{:S(2)}) async-start(bf16[48,8,1024]{2,0,1:T(8,128)(2,1)} %bitcast.44), calls=%async_computation | async-start | bytes 1572864 | tf_op jit(solution)/shard_map/all_to_all | solution.py:153
  31.1 0.9 copy-start.6
  32.0 4.5 %copy-start = (bf16[512,384]{1,0:T(8,128)(2,1)S(1)}, bf16[512,384]{1,0:T(8,128)(2,1)}, u32[]{:S(2)}) copy-start(bf16[512,384]{1,0:T(8,128)(2,1)} %user.1) | copy-start | bytes 1179652
  32.0 6.4 %copy-start.8 = (s32[2,3]{1,0:T(2,128)S(1)}, s32[2,3]{1,0:T(2,128)}, u32[]{:S(2)}) copy-start(s32[2,3]{1,0:T(2,128)} %param.9) | copy-start | bytes 76
  32.0 6.6 %copy-start.1 = (bf16[512,384]{1,0:T(8,128)(2,1)S(1)}, bf16[512,384]{1,0:T(8,128)(2,1)}, u32[]{:S(2)}) copy-start(bf16[512,384]{1,0:T(8,128)(2,1)} %item.1) | copy-start | bytes 1179652
  32.0 6.6 %copy-start.2 = (bf16[256,384]{1,0:T(8,128)(2,1)S(1)}, bf16[256,384]{1,0:T(8,128)(2,1)}, u32[]{:S(2)}) copy-start(bf16[256,384]{1,0:T(8,128)(2,1)} %week.1) | copy-start | bytes 589828
  32.0 6.6 %copy-start.3 = (s32[2]{0:T(128)S(1)}, s32[2]{0:T(128)}, u32[]{:S(2)}) copy-start(s32[2]{0:T(128)} %live.1) | copy-start | bytes 28
  32.0 52.4 %all-to-all-start.1 = ((bf16[128,8,1024]{2,0,1:T(8,128)(2,1)}), bf16[128,8,1024]{2,0,1:T(8,128)(2,1)}, u32[]{:S(2)}, u32[]{:S(2)}) async-start(bf16[128,8,1024]{2,0,1:T(8,128)(2,1)} %bitcast.46), calls=%async_computation.1 | async-start | bytes 4194304 | tf_op jit(solution)/shard_map/all_to_all | solution.py:156
  36.5 51.5 %collective-permute-start = (bf16[512,384]{1,0:T(8,128)(2,1)S(1)}, bf16[512,384]{1,0:T(8,128)(2,1)}, u32[]{:S(2)}, u32[]{:S(2)}) collective-permute-start(bf16[512,384]{1,0:T(8,128)(2,1)S(1)} %copy-done), channel_id=1, source_target_pairs={{0,16},{16,0},{1,17},{17,1},{2,18},{18,2},{3,19},{19,3},{4,20},{20... | collective-permute-start | bytes 1179656 | tf_op jit(solution)/shard_map/ppermute | solution.py:121
  84.4 19.4 %all-to-all-start.4 = ((f32[8,48,768]{2,1,0:T(8,128)}), f32[8,48,768]{2,1,0:T(8,128)S(1)}, u32[]{:S(2)}, u32[]{:S(2)}) async-start(f32[8,48,768]{2,1,0:T(8,128)} %reshape.40), calls=%async_computation.4 | async-start | bytes 2359296 | tf_op jit(solution)/shard_map/all_to_all | solution.py:131
  89.1 3.2 %copy-start.7 = (bf16[48,8,1024]{2,0,1:T(8,128)(2,1)S(1)}, bf16[48,8,1024]{2,0,1:T(8,128)(2,1)}, u32[]{:S(2)}) copy-start(bf16[48,8,1024]{2,0,1:T(8,128)(2,1)} %copy-done.6) | copy-start | bytes 2359300
  92.3 1.3 copy-start.5
  103.8 23.6 %all-to-all-start.2 = ((f32[4,8,32,384]{3,2,1,0:T(8,128)}), f32[4,8,32,384]{3,2,1,0:T(8,128)S(1)}, u32[]{:S(2)}, u32[]{:S(2)}) async-start(f32[4,8,32,384]{3,2,1,0:T(8,128)} %bitcast.43), calls=%async_computation.2 | async-start | bytes 3145728 | tf_op jit(solution)/shard_map/all_to_all | solution.py:131
  127.4 10.9 %all-to-all-start.5 = ((f32[4,12,768]{2,1,0:T(8,128)}), f32[4,12,768]{2,1,0:T(8,128)S(1)}, u32[]{:S(2)}, u32[]{:S(2)}) async-start(f32[4,12,768]{2,1,0:T(8,128)} %reshape.37), calls=%async_computation.5 | async-start | bytes 393216 | tf_op jit(solution)/shard_map/all_to_all | solution.py:131
  138.3 15.6 %all-to-all-start.3 = ((f32[8,32,384]{2,1,0:T(8,128)}), f32[8,32,384]{2,1,0:T(8,128)S(1)}, u32[]{:S(2)}, u32[]{:S(2)}) async-start(f32[8,32,384]{2,1,0:T(8,128)} %reduce_sum.36), calls=%async_computation.3 | async-start | bytes 786432 | tf_op jit(solution)/shard_map/all_to_all | solution.py:131
  153.9 39.9 %all-to-all-start.6 = ((f32[8,48,1024]{2,1,0:T(8,128)}), f32[8,48,1024]{2,1,0:T(8,128)S(1)}, u32[]{:S(2)}, u32[]{:S(2)}) async-start(f32[8,48,1024]{2,1,0:T(8,128)} %bitcast.10), calls=%async_computation.6 | async-start | bytes 3145728 | tf_op jit(solution)/shard_map/all_to_all | solution.py:180

commit v2 on v1

--- a/solution.py
+++ b/solution.py
@@ -127,8 +127,167 @@
     return whole
 
 
-def exchange(blocks, axes):
-    return lax.all_to_all(blocks, axes, split_axis=0, concat_axis=0, tiled=True)
+def peer(axes, shift):
+    size = 1
+    me = 0
+    for axis in axes:
+        size *= lax.axis_size(axis)
+        me = me * lax.axis_size(axis) + lax.axis_index(axis)
+    place = lax.rem(me + shift, size)
+    left = place
+    device = {}
+    for axis in reversed(axes):
+        device[axis] = lax.rem(left, lax.axis_size(axis))
+        left = left // lax.axis_size(axis)
+    return device, place
+
+
+def tail_kernel(
+    feat_in, user_in, both_in,
+    feat_out, user_out, item_out, week_out,
+    user_got, user_mid, user_last, both_got, both_mid, both_last,
+    own_sem, feat_sems, user_sems, last_sems, both_sems, item_sems,
+):
+    columns = ("user", "item")
+    sums = ("user", "feat")
+    n_columns = feat_in.shape[0]
+    n_feat = user_in.shape[0]
+    n_sums = both_in.shape[0]
+    n_item = both_mid.shape[0]
+    me_columns = peer(columns, 0)[1]
+    me_feat = lax.axis_index("feat")
+    me_sums = peer(sums, 0)[1]
+    me_item = lax.axis_index("item")
+
+    barrier = pltpu.get_barrier_semaphore()
+    for axes, count in ((columns, n_columns), (sums, n_sums)):
+        for shift in range(1, count):
+            pl.semaphore_signal(
+                barrier, inc=1, device_id=peer(axes, shift)[0],
+                device_id_type=pl.DeviceIdType.MESH,
+            )
+    pl.semaphore_wait(barrier, n_columns + n_sums - 2)
+
+    def send(src, dst, sems, shift, device):
+        copy = pltpu.make_async_remote_copy(
+            src_ref=src, dst_ref=dst, send_sem=sems.at[0, shift - 1],
+            recv_sem=sems.at[1, shift - 1], device_id=device,
+            device_id_type=pl.DeviceIdType.MESH,
+        )
+        copy.start()
+        return copy
+
+    both_copies = []
+    for shift in range(1, n_sums):
+        device, place = peer(sums, shift)
+        both_copies.append(
+            send(both_in.at[place], both_got.at[shift - 1], both_sems, shift, device)
+        )
+    user_copies = []
+    for shift in range(1, n_feat):
+        device, place = peer(("feat",), shift)
+        user_copies.append(
+            send(user_in.at[place], user_got.at[shift - 1], user_sems, shift, device)
+        )
+    width = feat_in.shape[2]
+    mine = pl.ds(pl.multiple_of(me_columns * width, width), width)
+    feat_copies = []
+    for shift in range(1, n_columns):
+        device, place = peer(columns, shift)
+        feat_copies.append(
+            send(feat_in.at[place], feat_out.at[:, mine], feat_sems, shift, device)
+        )
+    own = pltpu.make_async_copy(feat_in.at[me_columns], feat_out.at[:, mine], own_sem)
+    own.start()
+
+    for copy in both_copies:
+        copy.wait_recv()
+    total = both_in[me_sums]
+    for k in range(n_sums - 1):
+        total += both_got[k]
+    both_mid[...] = total
+    item_copies = []
+    for shift in range(1, n_item):
+        device, place = peer(("item",), shift)
+        item_copies.append(
+            send(both_mid.at[place], both_last.at[shift - 1], item_sems, shift, device)
+        )
+
+    for copy in user_copies:
+        copy.wait_recv()
+    total = user_in[me_feat]
+    for k in range(n_feat - 1):
+        total += user_got[k]
+    user_mid[...] = total
+    last_copies = []
+    for shift in range(1, n_columns):
+        device, place = peer(columns, shift)
+        last_copies.append(
+            send(user_mid.at[place], user_last.at[shift - 1], last_sems, shift, device)
+        )
+
+    item_rows = item_out.shape[2]
+    for copy in item_copies:
+        copy.wait_recv()
+    block = both_mid[me_item]
+    item_out[me_item] = block[:, :item_rows]
+    week = block[:, item_rows:]
+    for shift in range(1, n_item):
+        block = both_last[shift - 1]
+        item_out[lax.rem(me_item - shift + n_item, n_item)] = block[:, :item_rows]
+        week += block[:, item_rows:]
+    week_out[...] = week
+
+    for copy in last_copies:
+        copy.wait_recv()
+    total = user_mid[me_columns]
+    for k in range(n_columns - 1):
+        total += user_last[k]
+    user_out[...] = total
+
+    own.wait()
+    for copy in feat_copies:
+        copy.wait_recv()
+    for copy in both_copies + user_copies + feat_copies + item_copies + last_copies:
+        copy.wait_send()
+
+
+def tail(feat_in, user_in, both_in, item_rows):
+    n_columns, own_ranks, width = feat_in.shape
+    n_feat, _, rows, rank = user_in.shape
+    n_sums, n_item, own, length = both_in.shape
+    f32 = jnp.float32
+    vmem = pl.BlockSpec(memory_space=pltpu.VMEM)
+    pairs = lambda count: pltpu.SemaphoreType.DMA((2, count - 1))
+    return pl.pallas_call(
+        tail_kernel,
+        in_specs=[vmem] * 3,
+        out_specs=[vmem] * 4,
+        out_shape=[
+            jax.ShapeDtypeStruct((own_ranks, n_columns * width), f32),
+            jax.ShapeDtypeStruct((rows, rank), f32),
+            jax.ShapeDtypeStruct((n_item, own, item_rows), f32),
+            jax.ShapeDtypeStruct((own, length - item_rows), f32),
+        ],
+        scratch_shapes=[
+            pltpu.VMEM((n_feat - 1, n_columns, rows, rank), f32),
+            pltpu.VMEM((n_columns, rows, rank), f32),
+            pltpu.VMEM((n_columns - 1, rows, rank), f32),
+            pltpu.VMEM((n_sums - 1, n_item, own, length), f32),
+            pltpu.VMEM((n_item, own, length), f32),
+            pltpu.VMEM((n_item - 1, own, length), f32),
+            pltpu.SemaphoreType.DMA,
+            pairs(n_columns),
+            pairs(n_feat),
+            pairs(n_columns),
+            pairs(n_sums),
+            pairs(n_item),
+        ],
+        compiler_params=pltpu.CompilerParams(
+            collective_id=0, has_side_effects=True, vmem_limit_bytes=48 * 1024 * 1024
+        ),
+        name="tail_exchange",
+    )(feat_in, user_in, both_in)
 
 
 def local(
@@ -150,12 +309,13 @@
     own = rank // (n_user * n_item * n_feat)
     user_base = lax.axis_index("user") * user_rows
 
-    factor_cols = lax.all_to_all(
-        feat_factor, ("user", "item"), split_axis=1, concat_axis=0, tiled=True
-    )
-    side_cols = lax.all_to_all(
-        side_matrix, ("user", "item"), split_axis=1, concat_axis=0, tiled=True
-    )
+    side_rows = side_matrix.shape[0]
+    n_columns = n_user * n_item
+    sent = jnp.concatenate([side_matrix, feat_factor], axis=0)
+    got = lax.all_to_all(sent, ("user", "item"), split_axis=1, concat_axis=0, tiled=True)
+    got = got.reshape(n_columns, sent.shape[0], got.shape[1])
+    side_cols = got[:, :side_rows].reshape(n_columns * side_rows, got.shape[2])
+    factor_cols = got[:, side_rows:].reshape(rank, got.shape[2])
     all_users = gather_rows(user_factor, "user")
 
     user_sum, item_sum, week_sum = tile_sums(
@@ -165,19 +325,15 @@
     both = jnp.concatenate([item_sum, week_sum], axis=0).T
     both = both.reshape(n_user, n_item, n_feat, own, item_rows + week_rows)
     both = both.transpose(0, 2, 1, 3, 4).reshape(
-        n_user * n_feat, n_item * own, item_rows + week_rows
-    )
-    both = jnp.sum(exchange(both, ("user", "feat")), axis=0)
-    both = exchange(both.reshape(n_item, own, item_rows + week_rows), "item")
-    grad_item = both[:, :, :item_rows].transpose(0, 2, 1).reshape(n_item * item_rows, own)
-    grad_week = jnp.sum(both[:, :, item_rows:], axis=0).T
+        n_user * n_feat, n_item, own, item_rows + week_rows
+    )
 
     predicted = jnp.dot(all_users, factor_cols, preferred_element_type=jnp.float32)
     side_resid = (side_scale * (predicted - side_cols.astype(jnp.float32))).astype(jnp.bfloat16)
     feat_cols = lax.dot_general(
         all_users, side_resid, (((0,), (0,)), ((), ())), preferred_element_type=jnp.float32
     )
-    grad_feat = lax.all_to_all(feat_cols, ("user", "item"), split_axis=0, concat_axis=1, tiled=True)
+    feat_cols = feat_cols.reshape(n_columns, rank // n_columns, feat_cols.shape[1])
     side_user = lax.dot_general(
         side_resid, factor_cols, (((1,), (1,)), ((), ())), preferred_element_type=jnp.float32
     )
@@ -185,8 +341,9 @@
     user_total = lax.dynamic_update_slice_in_dim(side_user, mine + user_sum, user_base, 0)
     rows = user_total.shape[0] // (n_user * n_item * n_feat)
     by_feat = user_total.reshape(n_user * n_item, n_feat, rows, rank).transpose(1, 0, 2, 3)
-    by_feat = jnp.sum(exchange(by_feat, "feat"), axis=0)
-    grad_user = jnp.sum(exchange(by_feat, ("user", "item")), axis=0)
+    grad_feat, grad_user, by_item, by_week = tail(feat_cols, by_feat, both, item_rows)
+    grad_item = by_item.transpose(0, 2, 1).reshape(n_item * item_rows, own)
+    grad_week = by_week.T
     return (grad_user, grad_item, grad_week, grad_feat)
 
 

time: 197 us -> 140 us (0.71)
  the two profiles are of different devices: /device:TPU:0 before, /device:TPU:1 now
where the time goes in v2:
time: 140 us; the launch traced here: 138 us
  waiting for transfers between devices  55.2 us (39%)
  Pallas kernels  54.8 us (39%)
  local copies, waits for them, and re-layouts  13.4 us (10%)
  starting transfers between devices  7.96 us (6%)
  matrix products  3.51 us (3%)
  other arithmetic  2.49 us (2%)
    pallas_call x1, Pallas kernels, tail(): pl.pallas_call(tail_kernel, in_specs=[vmem] * 3, out_specs=[vmem] * 4, ou...  51.8 us
    all_to_all x1, waiting for transfers between devices, local(): lax.all_to_all(sent, ('user', 'item'), split_axis=1, concat_axis=0, tiled...  38.7 us
    ppermute x1, waiting for transfers between devices, gather_rows(): lax.ppermute(block, axis, [(k, (k + shift) % count) for k in range(count)])  16.5 us
    all_to_all x1, starting transfers between devices, local(): lax.all_to_all(sent, ('user', 'item'), split_axis=1, concat_axis=0, tiled...  6.5 us
    unnamed x15, local copies, waits for them, and re-layouts  3.11 us
    pallas_call x1, Pallas kernels, tile_sums(): pl.pallas_call(tile_kernel, grid_spec=pltpu.PrefetchScalarGridSpec(num_sc...  2.98 us
  transfers between devices with their start and end apart: 2, of which 2 were waited for; matrix products, arithmetic and copies ran while one was open for 4% of the time, Pallas kernels for 2%

profile of v2, /device:TPU:1, one launch (start us, length us, event | category | flops | bytes accessed | tf_op | source)
XLA Modules:
  0.0 138.1 jit_solution(14131970120206062114)
XLA Ops:
  0.6 2.1 %pad_maximum_fusion = bf16[176,8192]{1,0:T(8,128)(2,1)S(1)} fusion(bf16[48,8192]{1,0:T(8,128)(2,1)} %param.15, bf16[128,8192]{1,0:T(8,128)(2,1)} %param.11), kind=kLoop, calls=%fused_computation.4 | loop fusion | flops 5767168 | bytes 5767168 | tf_op jit(solution)/shard_map/concatenate | solution.py:314
  2.8 1.9 %copy.24 = bf16[22,8,8,1024]{3,2,0,1:T(8,128)(2,1)} copy(bf16[22,8,8,1024]{3,2,1,0:T(8,128)(2,1)S(1)} %bitcast.37) | data formatting | bytes 5767168 | tf_op jit(solution)/shard_map/all_to_all | solution.py:315
  4.7 0.0 copy-start.3
  4.7 6.5 %all-to-all-start = ((bf16[176,8,1024]{2,0,1:T(8,128)(2,1)}), bf16[176,8,1024]{2,0,1:T(8,128)(2,1)}, u32[]{:S(2)}, u32[]{:S(2)}) async-start(bf16[176,8,1024]{2,0,1:T(8,128)(2,1)} %bitcast.36), calls=%async_computation | async-start | bytes 5767168 | tf_op jit(solution)/shard_map/all_to_all | solution.py:315
  11.2 0.0 copy-done
  11.2 1.5 %collective-permute-start = (bf16[512,384]{1,0:T(8,128)(2,1)S(1)}, bf16[512,384]{1,0:T(8,128)(2,1)}, u32[]{:S(2)}, u32[]{:S(2)}) collective-permute-start(bf16[512,384]{1,0:T(8,128)(2,1)S(1)} %copy-done), channel_id=1, source_target_pairs={{0,16},{16,0},{1,17},{17,1},{2,18},{18,2},{3,19},{19,3},{4,20},{20... | collective-permute-start | bytes 1179656 | tf_op jit(solution)/shard_map/ppermute | solution.py:121
  12.7 0.0 copy-done.4
  12.7 0.1 compare_select_fusion.2
  12.8 0.1 pad_add_fusion.starts
  12.8 3.0 %tile_sums.1 = (f32[512,384]{1,0:T(8,128)S(1)}, f32[512,384]{1,0:T(8,128)S(1)}, f32[256,384]{1,0:T(8,128)S(1)}) custom-call(s32[2,3]{1,0:T(2,128)S(1)} %pad_add_fusion.starts, s32[2]{0:T(128)S(1)} %copy-done.3, bf16[2,256,16384]{2,1,0:T(8,128)(2,1)} %tile.1, bf16[512,384]{1,0:T(8,128)(2,1)S(1)} %copy-done, bf16[512,384]{1,0:T(8,128)(2,1)S(1)} %copy-done.1, ...), custom_call_target="tpu_custom_call" | custom-call | flops 19327352832 | bytes 16777216 | tf_op jit(solution)/shard_map/tile_sums/pallas_call | solution.py:86
  15.9 0.1 maximum_bitcast_fusion
  15.9 1.4 %copy.16 = f32[384,768]{1,0:T(8,128)} copy(f32[384,768]{0,1:T(8,128)S(1)} %maximum_bitcast_fusion) | data formatting | bytes 2359296 | tf_op jit(solution)/shard_map/transpose | solution.py:325
  17.3 1.4 reshape.37
  18.7 1.3 copy.17
  20.0 0.1 broadcast_in_dim.3
  20.1 0.1 constant_dynamic-update-slice_fusion.1
  20.1 16.5 %collective-permute-done = bf16[512,384]{1,0:T(8,128)(2,1)} collective-permute-done((bf16[512,384]{1,0:T(8,128)(2,1)S(1)}, bf16[512,384]{1,0:T(8,128)(2,1)}, u32[]{:S(2)}, u32[]{:S(2)}) %collective-permute-start) | collective-permute-done | bytes 393248 | tf_op jit(solution)/shard_map/ppermute | solution.py:121
  36.6 1.1 constant_dynamic-update-slice_fusion
  37.7 38.7 %all-to-all-done = bf16[176,8,1024]{2,0,1:T(8,128)(2,1)} async-done(((bf16[176,8,1024]{2,0,1:T(8,128)(2,1)}), bf16[176,8,1024]{2,0,1:T(8,128)(2,1)}, u32[]{:S(2)}, u32[]{:S(2)}) %all-to-all-start) | async-done | bytes 2883616 | tf_op jit(solution)/shard_map/all_to_all | solution.py:315
  76.4 1.8 %slice.21 = bf16[8,128,1024]{2,1,0:T(8,128)(2,1)S(1)} slice(bf16[8,176,1024]{2,1,0:T(8,128)(2,1)} %bitcast), slice={[0:8], [0:128], [0:1024]} | slice | bytes 4194304 | tf_op jit(solution)/shard_map/slice | solution.py:317
  78.2 1.2 slice.20
  79.4 1.2 fusion.1
  80.6 1.0 fusion.4
  81.6 1.3 fusion.5
  82.9 0.1 add_dynamic-update-slice_fusion
  83.0 0.1 copy.25
  83.1 51.8 %tail_exchange.1 = (f32[48,8192]{1,0:T(8,128)S(1)}, f32[32,384]{1,0:T(8,128)S(1)}, f32[4,12,512]{2,1,0:T(8,128)S(1)}, f32[12,256]{1,0:T(8,128)S(1)}) custom-call(f32[8,48,1024]{2,1,0:T(8,128)S(1)} %bitcast.32, f32[4,8,32,384]{3,2,1,0:T(8,128)S(1)} %bitcast.33, f32[8,4,12,768]{3,2,1,0:T(8,128)} %bitcast.38), custom_call_target="tpu_custom_call" | custom-call | tf_op jit(solution)/shard_map/tail_exchange/pallas_call | solution.py:262
  135.0 0.1 copy.26
  135.1 0.7 copy.20
  135.8 0.6 copy.33
  136.4 0.6 copy.34
  137.0 1.1 copy.35
  (8 shorter events, 0.0 us)
Async XLA Ops:
  4.7 6.5 %copy-start = (bf16[512,384]{1,0:T(8,128)(2,1)S(1)}, bf16[512,384]{1,0:T(8,128)(2,1)}, u32[]{:S(2)}) copy-start(bf16[512,384]{1,0:T(8,128)(2,1)} %user.1) | copy-start | bytes 1179652
  4.7 8.0 %copy-start.4 = (s32[2,3]{1,0:T(2,128)S(1)}, s32[2,3]{1,0:T(2,128)}, u32[]{:S(2)}) copy-start(s32[2,3]{1,0:T(2,128)} %param.9) | copy-start | bytes 76
  4.7 8.1 %copy-start.1 = (bf16[512,384]{1,0:T(8,128)(2,1)S(1)}, bf16[512,384]{1,0:T(8,128)(2,1)}, u32[]{:S(2)}) copy-start(bf16[512,384]{1,0:T(8,128)(2,1)} %item.1) | copy-start | bytes 1179652
  4.7 8.1 %copy-start.2 = (bf16[256,384]{1,0:T(8,128)(2,1)S(1)}, bf16[256,384]{1,0:T(8,128)(2,1)}, u32[]{:S(2)}) copy-start(bf16[256,384]{1,0:T(8,128)(2,1)} %week.1) | copy-start | bytes 589828
  4.7 8.1 %copy-start.3 = (s32[2]{0:T(128)S(1)}, s32[2]{0:T(128)}, u32[]{:S(2)}) copy-start(s32[2]{0:T(128)} %live.1) | copy-start | bytes 28
  4.7 71.7 %all-to-all-start = ((bf16[176,8,1024]{2,0,1:T(8,128)(2,1)}), bf16[176,8,1024]{2,0,1:T(8,128)(2,1)}, u32[]{:S(2)}, u32[]{:S(2)}) async-start(bf16[176,8,1024]{2,0,1:T(8,128)(2,1)} %bitcast.36), calls=%async_computation | async-start | bytes 5767168 | tf_op jit(solution)/shard_map/all_to_all | solution.py:315
  11.2 25.4 %collective-permute-start = (bf16[512,384]{1,0:T(8,128)(2,1)S(1)}, bf16[512,384]{1,0:T(8,128)(2,1)}, u32[]{:S(2)}, u32[]{:S(2)}) collective-permute-start(bf16[512,384]{1,0:T(8,128)(2,1)S(1)} %copy-done), channel_id=1, source_target_pairs={{0,16},{16,0},{1,17},{17,1},{2,18},{18,2},{3,19},{19,3},{4,20},{20... | collective-permute-start | bytes 1179656 | tf_op jit(solution)/shard_map/ppermute | solution.py:121

commit v3 on v2

--- a/solution.py
+++ b/solution.py
@@ -142,40 +142,38 @@
     return device, place
 
 
-def tail_kernel(
-    feat_in, user_in, both_in,
-    feat_out, user_out, item_out, week_out,
-    user_got, user_mid, user_last, both_got, both_mid, both_last,
-    own_sem, feat_sems, user_sems, last_sems, both_sems, item_sems,
-):
-    columns = ("user", "item")
-    sums = ("user", "feat")
-    n_columns = feat_in.shape[0]
-    n_feat = user_in.shape[0]
-    n_sums = both_in.shape[0]
-    n_item = both_mid.shape[0]
-    me_columns = peer(columns, 0)[1]
-    me_feat = lax.axis_index("feat")
-    me_sums = peer(sums, 0)[1]
-    me_item = lax.axis_index("item")
-
+def greet(groups):
     barrier = pltpu.get_barrier_semaphore()
-    for axes, count in ((columns, n_columns), (sums, n_sums)):
+    expected = 0
+    for axes, count in groups:
         for shift in range(1, count):
             pl.semaphore_signal(
                 barrier, inc=1, device_id=peer(axes, shift)[0],
                 device_id_type=pl.DeviceIdType.MESH,
             )
-    pl.semaphore_wait(barrier, n_columns + n_sums - 2)
-
-    def send(src, dst, sems, shift, device):
-        copy = pltpu.make_async_remote_copy(
-            src_ref=src, dst_ref=dst, send_sem=sems.at[0, shift - 1],
-            recv_sem=sems.at[1, shift - 1], device_id=device,
-            device_id_type=pl.DeviceIdType.MESH,
-        )
-        copy.start()
-        return copy
+        expected += count - 1
+    pl.semaphore_wait(barrier, expected)
+
+
+def send(src, dst, sems, shift, device):
+    copy = pltpu.make_async_remote_copy(
+        src_ref=src, dst_ref=dst, send_sem=sems.at[0, shift - 1],
+        recv_sem=sems.at[1, shift - 1], device_id=device,
+        device_id_type=pl.DeviceIdType.MESH,
+    )
+    copy.start()
+    return copy
+
+
+def item_kernel(
+    both_in, item_out, week_out, both_got, both_mid, both_last, both_sems, item_sems
+):
+    sums = ("user", "feat")
+    n_sums = both_in.shape[0]
+    n_item = both_mid.shape[0]
+    me_sums = peer(sums, 0)[1]
+    me_item = lax.axis_index("item")
+    greet(((sums, n_sums), (("item",), n_item)))
 
     both_copies = []
     for shift in range(1, n_sums):
@@ -183,23 +181,6 @@
         both_copies.append(
             send(both_in.at[place], both_got.at[shift - 1], both_sems, shift, device)
         )
-    user_copies = []
-    for shift in range(1, n_feat):
-        device, place = peer(("feat",), shift)
-        user_copies.append(
-            send(user_in.at[place], user_got.at[shift - 1], user_sems, shift, device)
-        )
-    width = feat_in.shape[2]
-    mine = pl.ds(pl.multiple_of(me_columns * width, width), width)
-    feat_copies = []
-    for shift in range(1, n_columns):
-        device, place = peer(columns, shift)
-        feat_copies.append(
-            send(feat_in.at[place], feat_out.at[:, mine], feat_sems, shift, device)
-        )
-    own = pltpu.make_async_copy(feat_in.at[me_columns], feat_out.at[:, mine], own_sem)
-    own.start()
-
     for copy in both_copies:
         copy.wait_recv()
     total = both_in[me_sums]
@@ -212,6 +193,46 @@
         item_copies.append(
             send(both_mid.at[place], both_last.at[shift - 1], item_sems, shift, device)
         )
+    item_rows = item_out.shape[2]
+    for copy in item_copies:
+        copy.wait_recv()
+    block = both_mid[me_item]
+    item_out[me_item] = block[:, :item_rows]
+    week = block[:, item_rows:]
+    for shift in range(1, n_item):
+        block = both_last[shift - 1]
+        item_out[lax.rem(me_item - shift + n_item, n_item)] = block[:, :item_rows]
+        week += block[:, item_rows:]
+    week_out[...] = week
+    for copy in both_copies + item_copies:
+        copy.wait_send()
+
+
+def tail_kernel(
+    scale_in, user_in, scale_out, user_out,
+    user_got, user_mid, user_last, own_sem, scale_sems, user_sems, last_sems,
+):
+    columns = ("user", "item")
+    n_columns = scale_out.shape[0]
+    n_feat = user_in.shape[0]
+    me_columns = peer(columns, 0)[1]
+    me_feat = lax.axis_index("feat")
+    greet(((columns, n_columns), (("feat",), n_feat)))
+
+    user_copies = []
+    for shift in range(1, n_feat):
+        device, place = peer(("feat",), shift)
+        user_copies.append(
+            send(user_in.at[place], user_got.at[shift - 1], user_sems, shift, device)
+        )
+    scale_copies = []
+    for shift in range(1, n_columns):
+        device, place = peer(columns, shift)
+        scale_copies.append(
+            send(scale_in, scale_out.at[me_columns], scale_sems, shift, device)
+        )
+    own = pltpu.make_async_copy(scale_in, scale_out.at[me_columns], own_sem)
+    own.start()
 
     for copy in user_copies:
         copy.wait_recv()
@@ -225,19 +246,6 @@
         last_copies.append(
             send(user_mid.at[place], user_last.at[shift - 1], last_sems, shift, device)
         )
-
-    item_rows = item_out.shape[2]
-    for copy in item_copies:
-        copy.wait_recv()
-    block = both_mid[me_item]
-    item_out[me_item] = block[:, :item_rows]
-    week = block[:, item_rows:]
-    for shift in range(1, n_item):
-        block = both_last[shift - 1]
-        item_out[lax.rem(me_item - shift + n_item, n_item)] = block[:, :item_rows]
-        week += block[:, item_rows:]
-    week_out[...] = week
-
     for copy in last_copies:
         copy.wait_recv()
     total = user_mid[me_columns]
@@ -246,48 +254,78 @@
     user_out[...] = total
 
     own.wait()
-    for copy in feat_copies:
+    for copy in scale_copies:
         copy.wait_recv()
-    for copy in both_copies + user_copies + feat_copies + item_copies + last_copies:
+    for copy in user_copies + scale_copies + last_copies:
         copy.wait_send()
 
 
-def tail(feat_in, user_in, both_in, item_rows):
-    n_columns, own_ranks, width = feat_in.shape
-    n_feat, _, rows, rank = user_in.shape
+def pair_sems(count):
+    return pltpu.SemaphoreType.DMA((2, count - 1))
+
+
+def item_exchange(both_in, item_rows):
     n_sums, n_item, own, length = both_in.shape
     f32 = jnp.float32
     vmem = pl.BlockSpec(memory_space=pltpu.VMEM)
-    pairs = lambda count: pltpu.SemaphoreType.DMA((2, count - 1))
+    return pl.pallas_call(
+        item_kernel,
+        in_specs=[vmem],
+        out_specs=[vmem] * 2,
+        out_shape=[
+            jax.ShapeDtypeStruct((n_item, own, item_rows), f32),
+            jax.ShapeDtypeStruct((own, length - item_rows), f32),
+        ],
+        scratch_shapes=[
+            pltpu.VMEM((n_sums - 1, n_item, own, length), f32),
+            pltpu.VMEM((n_item, own, length), f32),
+            pltpu.VMEM((n_item - 1, own, length), f32),
+            pair_sems(n_sums),
+            pair_sems(n_item),
+        ],
+        compiler_params=pltpu.CompilerParams(
+            collective_id=1, has_side_effects=True, vmem_limit_bytes=32 * 1024 * 1024
+        ),
+        cost_estimate=pl.CostEstimate(
+            flops=10**9, bytes_accessed=40 * 10**6, transcendentals=0
+        ),
+        name="item_exchange",
+    )(both_in)
+
+
+def tail(scale_in, user_in):
+    n_feat, n_columns, rows, rank = user_in.shape
+    f32 = jnp.float32
+    vmem = pl.BlockSpec(memory_space=pltpu.VMEM)
     return pl.pallas_call(
         tail_kernel,
-        in_specs=[vmem] * 3,
-        out_specs=[vmem] * 4,
+        in_specs=[vmem] * 2,
+        out_specs=[vmem] * 2,
         out_shape=[
-            jax.ShapeDtypeStruct((own_ranks, n_columns * width), f32),
+            jax.ShapeDtypeStruct((n_columns,) + scale_in.shape, f32),
             jax.ShapeDtypeStruct((rows, rank), f32),
-            jax.ShapeDtypeStruct((n_item, own, item_rows), f32),
-            jax.ShapeDtypeStruct((own, length - item_rows), f32),
         ],
         scratch_shapes=[
             pltpu.VMEM((n_feat - 1, n_columns, rows, rank), f32),
             pltpu.VMEM((n_columns, rows, rank), f32),
             pltpu.VMEM((n_columns - 1, rows, rank), f32),
-            pltpu.VMEM((n_sums - 1, n_item, own, length), f32),
-            pltpu.VMEM((n_item, own, length), f32),
-            pltpu.VMEM((n_item - 1, own, length), f32),
             pltpu.SemaphoreType.DMA,
-            pairs(n_columns),
-            pairs(n_feat),
-            pairs(n_columns),
-            pairs(n_sums),
-            pairs(n_item),
+            pair_sems(n_columns),
+            pair_sems(n_feat),
+            pair_sems(n_columns),
         ],
         compiler_params=pltpu.CompilerParams(
             collective_id=0, has_side_effects=True, vmem_limit_bytes=48 * 1024 * 1024
         ),
+        cost_estimate=pl.CostEstimate(
+            flops=10**9, bytes_accessed=80 * 10**6, transcendentals=0
+        ),
         name="tail_exchange",
-    )(feat_in, user_in, both_in)
+    )(scale_in, user_in)
+
+
+def exchange(blocks, axes):
+    return lax.all_to_all(blocks, axes, split_axis=0, concat_axis=0, tiled=True)
 
 
 def local(
@@ -313,9 +351,6 @@
     n_columns = n_user * n_item
     sent = jnp.concatenate([side_matrix, feat_factor], axis=0)
     got = lax.all_to_all(sent, ("user", "item"), split_axis=1, concat_axis=0, tiled=True)
-    got = got.reshape(n_columns, sent.shape[0], got.shape[1])
-    side_cols = got[:, :side_rows].reshape(n_columns * side_rows, got.shape[2])
-    factor_cols = got[:, side_rows:].reshape(rank, got.shape[2])
     all_users = gather_rows(user_factor, "user")
 
     user_sum, item_sum, week_sum = tile_sums(
@@ -327,13 +362,24 @@
     both = both.transpose(0, 2, 1, 3, 4).reshape(
         n_user * n_feat, n_item, own, item_rows + week_rows
     )
+    by_item, by_week = item_exchange(both, item_rows)
+    got, by_item, by_week, user_sum = lax.optimization_barrier((got, by_item, by_week, user_sum))
+    got = got.reshape(n_columns, sent.shape[0], got.shape[1])
+    side_cols = got[:, :side_rows].reshape(n_columns * side_rows, got.shape[2])
+    factor_cols = got[:, side_rows:].reshape(rank, got.shape[2])
+    grad_item = by_item.transpose(0, 2, 1).reshape(n_item * item_rows, own)
+    grad_week = by_week.T
 
     predicted = jnp.dot(all_users, factor_cols, preferred_element_type=jnp.float32)
     side_resid = (side_scale * (predicted - side_cols.astype(jnp.float32))).astype(jnp.bfloat16)
     feat_cols = lax.dot_general(
         all_users, side_resid, (((0,), (0,)), ((), ())), preferred_element_type=jnp.float32
     )
-    feat_cols = feat_cols.reshape(n_columns, rank // n_columns, feat_cols.shape[1])
+    width = feat_cols.shape[1]
+    scale = jnp.maximum(jnp.max(jnp.abs(feat_cols)), 1e-30) / 16384.0
+    own_ranks = rank // n_columns
+    coded = (feat_cols * (1.0 / scale)).astype(jnp.float16)
+    coded = exchange(coded.reshape(n_columns, own_ranks, width), ("user", "item"))
     side_user = lax.dot_general(
         side_resid, factor_cols, (((1,), (1,)), ((), ())), preferred_element_type=jnp.float32
     )
@@ -341,9 +387,12 @@
     user_total = lax.dynamic_update_slice_in_dim(side_user, mine + user_sum, user_base, 0)
     rows = user_total.shape[0] // (n_user * n_item * n_feat)
     by_feat = user_total.reshape(n_user * n_item, n_feat, rows, rank).transpose(1, 0, 2, 3)
-    grad_feat, grad_user, by_item, by_week = tail(feat_cols, by_feat, both, item_rows)
-    grad_item = by_item.transpose(0, 2, 1).reshape(n_item * item_rows, own)
-    grad_week = by_week.T
+    scales, grad_user = tail(jnp.full((8, 128), scale), by_feat)
+    grad_feat = (
+        (coded.astype(jnp.float32) * scales[:, :1, :1])
+        .transpose(1, 0, 2)
+        .reshape(own_ranks, n_columns * width)
+    )
     return (grad_user, grad_item, grad_week, grad_feat)
 
 

time: 140 us -> 142 us (1.014)
  waiting for transfers between devices: 55.2 us -> 0.01 us
  Pallas kernels: 54.8 us -> 102 us
  matrix products: 3.51 us -> 7.47 us
  starting transfers between devices: 7.96 us -> 11.6 us
    pallas_call x1 -> x2, Pallas kernels: 51.8 us -> 99.3 us  [the longest x1 66.9 us: item_exchange(): pl.pallas_call(item_kernel, in_specs=[vmem], out_specs=[vmem] * 2, out_sh...]
    all_to_all x1, waiting for transfers between devices: 38.7 us -> 0.01 us  [local(): lax.all_to_all(sent, ('user', 'item'), split_axis=1, concat_axis=0, tiled...]
    ppermute x1, waiting for transfers between devices: 16.5 us -> 0.01 us  [gather_rows(): lax.ppermute(block, axis, [(k, (k + shift) % count) for k in range(count)])]
    all_to_all x0 -> x1, starting transfers between devices: none -> 3.68 us  [exchange(): return lax.all_to_all(blocks, axes, split_axis=0, concat_axis=0, tiled=True)]
    dot_general x1, matrix products: 1 us -> 3.36 us  [local(): lax.dot_general(all_users, side_resid, (((0,), (0,)), ((), ())), preferre...]
    dot_general x1, matrix products: 1.27 us -> 2.86 us  [local(): lax.dot_general(side_resid, factor_cols, (((1,), (1,)), ((), ())), prefer...]
    unnamed x15 -> x22, local copies, waits for them, and re-layouts: 3.11 us -> 1.98 us
  transfers between devices with their start and end apart: 2 -> 3, of which waited for: 2 -> 0; matrix products, arithmetic and copies ran while one was open for 4% -> 6% of each run, Pallas kernels for 2% -> 73%
where the time goes in v3:
time: 142 us; the launch traced here: 140 us
  Pallas kernels  102 us (72%)
  local copies, waits for them, and re-layouts  13.4 us (9%)
  starting transfers between devices  11.6 us (8%)
  matrix products  7.47 us (5%)
  other arithmetic  3.86 us (3%)
  between operations  1.58 us (1%)
    pallas_call x1, Pallas kernels, item_exchange(): pl.pallas_call(item_kernel, in_specs=[vmem], out_specs=[vmem] * 2, out_sh...  66.9 us
    pallas_call x1, Pallas kernels, tail(): pl.pallas_call(tail_kernel, in_specs=[vmem] * 2, out_specs=[vmem] * 2, ou...  32.4 us
    all_to_all x1, starting transfers between devices, local(): lax.all_to_all(sent, ('user', 'item'), split_axis=1, concat_axis=0, tiled...  6.5 us
    all_to_all x1, starting transfers between devices, exchange(): return lax.all_to_all(blocks, axes, split_axis=0, concat_axis=0, tiled=True)  3.68 us
    dot_general x1, matrix products, local(): lax.dot_general(all_users, side_resid, (((0,), (0,)), ((), ())), preferre...  3.36 us
    pallas_call x1, Pallas kernels, tile_sums(): pl.pallas_call(tile_kernel, grid_spec=pltpu.PrefetchScalarGridSpec(num_sc...  2.98 us
    dot_general x1, matrix products, local(): lax.dot_general(side_resid, factor_cols, (((1,), (1,)), ((), ())), prefer...  2.86 us
  transfers between devices with their start and end apart: 3, of which 0 were waited for; matrix products, arithmetic and copies ran while one was open for 6% of the time, Pallas kernels for 73%

profile of v3, /device:TPU:1, one launch (start us, length us, event | category | flops | bytes accessed | tf_op | source)
XLA Modules:
  0.0 140.3 jit_solution(1450279674103266809)
XLA Ops:
  0.6 2.1 %pad_maximum_fusion = bf16[176,8192]{1,0:T(8,128)(2,1)S(1)} fusion(bf16[48,8192]{1,0:T(8,128)(2,1)} %param.15, bf16[128,8192]{1,0:T(8,128)(2,1)} %param.11), kind=kLoop, calls=%fused_computation.4 | loop fusion | flops 5767168 | bytes 5767168 | tf_op jit(solution)/shard_map/concatenate | solution.py:352
  2.8 1.9 %copy.37 = bf16[22,8,8,1024]{3,2,0,1:T(8,128)(2,1)} copy(bf16[22,8,8,1024]{3,2,1,0:T(8,128)(2,1)S(1)} %bitcast.44) | data formatting | bytes 5767168 | tf_op jit(solution)/shard_map/all_to_all | solution.py:353
  4.7 6.5 %all-to-all-start = ((bf16[176,8,1024]{2,0,1:T(8,128)(2,1)}), bf16[176,8,1024]{2,0,1:T(8,128)(2,1)}, u32[]{:S(2)}, u32[]{:S(2)}) async-start(bf16[176,8,1024]{2,0,1:T(8,128)(2,1)} %bitcast.43), calls=%async_computation | async-start | bytes 5767168 | tf_op jit(solution)/shard_map/all_to_all | solution.py:353
  11.2 1.5 %collective-permute-start = (bf16[512,384]{1,0:T(8,128)(2,1)S(1)}, bf16[512,384]{1,0:T(8,128)(2,1)}, u32[]{:S(2)}, u32[]{:S(2)}) collective-permute-start(bf16[512,384]{1,0:T(8,128)(2,1)S(1)} %copy-done), channel_id=1, source_target_pairs={{0,16},{16,0},{1,17},{17,1},{2,18},{18,2},{3,19},{19,3},{4,20},{20... | collective-permute-start | bytes 1179656 | tf_op jit(solution)/shard_map/ppermute | solution.py:121
  12.7 0.1 compare_select_fusion.2
  12.7 0.1 pad_add_fusion.starts
  12.8 3.0 %tile_sums.1 = (f32[512,384]{1,0:T(8,128)S(1)}, f32[512,384]{1,0:T(8,128)S(1)}, f32[256,384]{1,0:T(8,128)S(1)}) custom-call(s32[2,3]{1,0:T(2,128)S(1)} %pad_add_fusion.starts, s32[2]{0:T(128)S(1)} %copy-done.3, bf16[2,256,16384]{2,1,0:T(8,128)(2,1)} %tile.1, bf16[512,384]{1,0:T(8,128)(2,1)S(1)} %copy-done, bf16[512,384]{1,0:T(8,128)(2,1)S(1)} %copy-done.1, ...), custom_call_target="tpu_custom_call" | custom-call | flops 19327352832 | bytes 16777216 | tf_op jit(solution)/shard_map/tile_sums/pallas_call | solution.py:86
  15.8 0.1 maximum_bitcast_fusion
  15.9 0.4 copy.26
  16.3 1.3 reshape.38
  17.6 1.5 %copy.27 = f32[2,4,4,12,768]{4,3,2,1,0:T(8,128)S(1)} copy(f32[2,4,4,12,768]{4,3,1,2,0:T(8,128)} %bitcast.45) | data formatting | bytes 2359296 | tf_op jit(solution)/shard_map/transpose | solution.py:362
  19.1 66.9 %item_exchange.1 = (f32[4,12,512]{2,1,0:T(8,128)S(1)}, f32[12,256]{1,0:T(8,128)S(1)}) custom-call(f32[8,4,12,768]{3,2,1,0:T(8,128)S(1)} %bitcast.39), custom_call_target="tpu_custom_call" | custom-call | flops 1000000000 | bytes 40000000 | tf_op jit(solution)/shard_map/item_exchange/pallas_call | solution.py:271
  86.0 0.1 broadcast_in_dim.6
  86.1 0.1 constant_dynamic-update-slice_fusion.1
  86.2 1.1 constant_dynamic-update-slice_fusion
  87.3 1.5 %slice.24 = bf16[8,48,1024]{2,1,0:T(8,128)(2,1)S(1)} slice(bf16[8,176,1024]{2,1,0:T(8,128)(2,1)} %bitcast.5), slice={[0:8], [128:176], [0:1024]} | slice | bytes 1572864 | tf_op jit(solution)/shard_map/slice | solution.py:369
  88.8 2.1 %slice.25 = bf16[8,128,1024]{2,1,0:T(8,128)(2,1)S(1)} slice(bf16[8,176,1024]{2,1,0:T(8,128)(2,1)} %bitcast.5), slice={[0:8], [0:128], [0:1024]} | slice | bytes 4194304 | tf_op jit(solution)/shard_map/slice | solution.py:368
  90.9 1.3 fusion.1
  92.1 3.4 %abs_reduce_fusion = (f32[]{:T(128)}, f32[384,1024]{1,0:T(8,128)S(1)}) fusion(bf16[1024,384]{1,0:T(8,128)(2,1)} %copy-done.4, bf16[1024,1024]{1,0:T(8,128)(2,1)S(1)} %fusion.1), kind=kOutput, calls=%fused_computation.8 | convolution fusion | flops 806092800 | bytes 4456452 | tf_op jit(solution)/shard_map/dot_general | solution.py:375
  96.2 1.1 multiply_convert_fusion
  97.3 3.7 %all-to-all-start.1 = ((f16[8,48,1024]{2,1,0:T(8,128)(2,1)}), f16[8,48,1024]{2,1,0:T(8,128)(2,1)S(1)}, u32[]{:S(2)}, u32[]{:S(2)}) async-start(f16[8,48,1024]{2,1,0:T(8,128)(2,1)} %bitcast.47), calls=%async_computation.1 | async-start | bytes 1572864 | tf_op jit(solution)/shard_map/all_to_all | solution.py:328
  101.0 0.1 copy.39
  101.1 0.7 copy.33
  101.8 2.9 %fusion.4 = f32[1024,384]{1,0:T(8,128)S(1)} fusion(bf16[1024,1024]{1,0:T(8,128)(2,1)} %copy-done.5, bf16[384,1024]{1,0:T(8,128)(2,1)S(1)} %bitcast.51), kind=kOutput, calls=%fused_computation.23 | convolution fusion | flops 805306368 | bytes 4456448 | tf_op jit(solution)/shard_map/dot_general | solution.py:383
  104.6 0.1 add_dynamic-update-slice_fusion
  104.8 0.1 copy.38
  104.9 32.4 %tail_exchange.1 = (f32[8,8,128]{2,1,0:T(8,128)S(1)}, f32[32,384]{1,0:T(8,128)S(1)}) custom-call(f32[8,128]{1,0:T(8,128)S(1)} %broadcast_in_dim.7.scale_in, f32[4,8,32,384]{3,2,1,0:T(8,128)S(1)} %bitcast.40), custom_call_target="tpu_custom_call" | custom-call | flops 1000000000 | bytes 80000000 | tf_op jit(solution)/shard_map/tail_exchange/pallas_call | solution.py:300
  137.3 0.1 slice_reduce_fusion
  137.5 0.3 multiply_bitcast_fusion
  137.8 1.3 copy.32
  139.0 0.6 copy.45
  139.6 0.6 copy.46
  (23 shorter events, 0.1 us)
Async XLA Ops:
  4.7 6.5 %copy-start = (bf16[512,384]{1,0:T(8,128)(2,1)S(1)}, bf16[512,384]{1,0:T(8,128)(2,1)}, u32[]{:S(2)}) copy-start(bf16[512,384]{1,0:T(8,128)(2,1)} %user.1) | copy-start | bytes 1179652
  4.7 8.0 %copy-start.8 = (s32[2,3]{1,0:T(2,128)S(1)}, s32[2,3]{1,0:T(2,128)}, u32[]{:S(2)}) copy-start(s32[2,3]{1,0:T(2,128)} %param.9) | copy-start | bytes 76
  4.7 8.1 %copy-start.1 = (bf16[512,384]{1,0:T(8,128)(2,1)S(1)}, bf16[512,384]{1,0:T(8,128)(2,1)}, u32[]{:S(2)}) copy-start(bf16[512,384]{1,0:T(8,128)(2,1)} %item.1) | copy-start | bytes 1179652
  4.7 8.1 %copy-start.2 = (bf16[256,384]{1,0:T(8,128)(2,1)S(1)}, bf16[256,384]{1,0:T(8,128)(2,1)}, u32[]{:S(2)}) copy-start(bf16[256,384]{1,0:T(8,128)(2,1)} %week.1) | copy-start | bytes 589828
  4.7 8.1 %copy-start.3 = (s32[2]{0:T(128)S(1)}, s32[2]{0:T(128)}, u32[]{:S(2)}) copy-start(s32[2]{0:T(128)} %live.1) | copy-start | bytes 28
  4.7 82.6 %all-to-all-start = ((bf16[176,8,1024]{2,0,1:T(8,128)(2,1)}), bf16[176,8,1024]{2,0,1:T(8,128)(2,1)}, u32[]{:S(2)}, u32[]{:S(2)}) async-start(bf16[176,8,1024]{2,0,1:T(8,128)(2,1)} %bitcast.43), calls=%async_computation | async-start | bytes 5767168 | tf_op jit(solution)/shard_map/all_to_all | solution.py:353
  11.2 75.0 %collective-permute-start = (bf16[512,384]{1,0:T(8,128)(2,1)S(1)}, bf16[512,384]{1,0:T(8,128)(2,1)}, u32[]{:S(2)}, u32[]{:S(2)}) collective-permute-start(bf16[512,384]{1,0:T(8,128)(2,1)S(1)} %copy-done), channel_id=1, source_target_pairs={{0,16},{16,0},{1,17},{17,1},{2,18},{18,2},{3,19},{19,3},{4,20},{20... | collective-permute-start | bytes 1179656 | tf_op jit(solution)/shard_map/ppermute | solution.py:121
  87.3 3.6 %copy-start.4 = (bf16[1024,384]{1,0:T(8,128)(2,1)}, bf16[1024,384]{1,0:T(8,128)(2,1)S(1)}, u32[]{:S(2)}) copy-start(bf16[1024,384]{1,0:T(8,128)(2,1)S(1)} %constant_dynamic-update-slice_fusion) | copy-start | bytes 2359300
  88.8 2.1 %copy-start.6 = (bf16[8,48,1024]{2,1,0:T(8,128)(2,1)}, bf16[8,48,1024]{2,1,0:T(8,128)(2,1)S(1)}, u32[]{:S(2)}) copy-start(bf16[8,48,1024]{2,1,0:T(8,128)(2,1)S(1)} %slice.24) | copy-start | bytes 2359300
  92.1 3.4 %copy-start.5 = (bf16[1024,1024]{1,0:T(8,128)(2,1)}, bf16[1024,1024]{1,0:T(8,128)(2,1)S(1)}, u32[]{:S(2)}) copy-start(bf16[1024,1024]{1,0:T(8,128)(2,1)S(1)} %fusion.1) | copy-start | bytes 6291460
  97.3 4.5 %copy-start.7 = (bf16[8,48,1024]{2,1,0:T(8,128)(2,1)S(1)}, bf16[8,48,1024]{2,1,0:T(8,128)(2,1)}, u32[]{:S(2)}) copy-start(bf16[8,48,1024]{2,1,0:T(8,128)(2,1)} %copy-done.6) | copy-start | bytes 2359300
  97.3 40.2 %all-to-all-start.1 = ((f16[8,48,1024]{2,1,0:T(8,128)(2,1)}), f16[8,48,1024]{2,1,0:T(8,128)(2,1)S(1)}, u32[]{:S(2)}, u32[]{:S(2)}) async-start(f16[8,48,1024]{2,1,0:T(8,128)(2,1)} %bitcast.47), calls=%async_computation.1 | async-start | bytes 1572864 | tf_op jit(solution)/shard_map/all_to_all | solution.py:328

commit v4 on v2

--- a/solution.py
+++ b/solution.py
@@ -143,14 +143,14 @@
 
 
 def tail_kernel(
-    feat_in, user_in, both_in,
-    feat_out, user_out, item_out, week_out,
+    scale_in, user_in, both_in,
+    scale_out, user_out, item_out, week_out,
     user_got, user_mid, user_last, both_got, both_mid, both_last,
-    own_sem, feat_sems, user_sems, last_sems, both_sems, item_sems,
+    own_sem, scale_sems, user_sems, last_sems, both_sems, item_sems,
 ):
     columns = ("user", "item")
     sums = ("user", "feat")
-    n_columns = feat_in.shape[0]
+    n_columns = scale_out.shape[0]
     n_feat = user_in.shape[0]
     n_sums = both_in.shape[0]
     n_item = both_mid.shape[0]
@@ -177,28 +177,39 @@
         copy.start()
         return copy
 
+    user_copies = []
+    for shift in range(1, n_feat):
+        device, place = peer(("feat",), shift)
+        user_copies.append(
+            send(user_in.at[place], user_got.at[shift - 1], user_sems, shift, device)
+        )
     both_copies = []
     for shift in range(1, n_sums):
         device, place = peer(sums, shift)
         both_copies.append(
             send(both_in.at[place], both_got.at[shift - 1], both_sems, shift, device)
         )
-    user_copies = []
-    for shift in range(1, n_feat):
-        device, place = peer(("feat",), shift)
-        user_copies.append(
-            send(user_in.at[place], user_got.at[shift - 1], user_sems, shift, device)
-        )
-    width = feat_in.shape[2]
-    mine = pl.ds(pl.multiple_of(me_columns * width, width), width)
-    feat_copies = []
+    scale_copies = []
     for shift in range(1, n_columns):
         device, place = peer(columns, shift)
-        feat_copies.append(
-            send(feat_in.at[place], feat_out.at[:, mine], feat_sems, shift, device)
-        )
-    own = pltpu.make_async_copy(feat_in.at[me_columns], feat_out.at[:, mine], own_sem)
+        scale_copies.append(
+            send(scale_in, scale_out.at[me_columns], scale_sems, shift, device)
+        )
+    own = pltpu.make_async_copy(scale_in, scale_out.at[me_columns], own_sem)
     own.start()
+
+    for copy in user_copies:
+        copy.wait_recv()
+    total = user_in[me_feat]
+    for k in range(n_feat - 1):
+        total += user_got[k]
+    user_mid[...] = total
+    last_copies = []
+    for shift in range(1, n_columns):
+        device, place = peer(columns, shift)
+        last_copies.append(
+            send(user_mid.at[place], user_last.at[shift - 1], last_sems, shift, device)
+        )
 
     for copy in both_copies:
         copy.wait_recv()
@@ -213,19 +224,6 @@
             send(both_mid.at[place], both_last.at[shift - 1], item_sems, shift, device)
         )
 
-    for copy in user_copies:
-        copy.wait_recv()
-    total = user_in[me_feat]
-    for k in range(n_feat - 1):
-        total += user_got[k]
-    user_mid[...] = total
-    last_copies = []
-    for shift in range(1, n_columns):
-        device, place = peer(columns, shift)
-        last_copies.append(
-            send(user_mid.at[place], user_last.at[shift - 1], last_sems, shift, device)
-        )
-
     item_rows = item_out.shape[2]
     for copy in item_copies:
         copy.wait_recv()
@@ -246,15 +244,14 @@
     user_out[...] = total
 
     own.wait()
-    for copy in feat_copies:
-        copy.wait_recv()
-    for copy in both_copies + user_copies + feat_copies + item_copies + last_copies:
+    for copy in scale_copies:
+        copy.wait_recv()
+    for copy in both_copies + user_copies + scale_copies + item_copies + last_copies:
         copy.wait_send()
 
 
-def tail(feat_in, user_in, both_in, item_rows):
-    n_columns, own_ranks, width = feat_in.shape
-    n_feat, _, rows, rank = user_in.shape
+def tail(scale_in, user_in, both_in, item_rows):
+    n_feat, n_columns, rows, rank = user_in.shape
     n_sums, n_item, own, length = both_in.shape
     f32 = jnp.float32
     vmem = pl.BlockSpec(memory_space=pltpu.VMEM)
@@ -264,7 +261,7 @@
         in_specs=[vmem] * 3,
         out_specs=[vmem] * 4,
         out_shape=[
-            jax.ShapeDtypeStruct((own_ranks, n_columns * width), f32),
+            jax.ShapeDtypeStruct((n_columns,) + scale_in.shape, f32),
             jax.ShapeDtypeStruct((rows, rank), f32),
             jax.ShapeDtypeStruct((n_item, own, item_rows), f32),
             jax.ShapeDtypeStruct((own, length - item_rows), f32),
@@ -286,8 +283,15 @@
         compiler_params=pltpu.CompilerParams(
             collective_id=0, has_side_effects=True, vmem_limit_bytes=48 * 1024 * 1024
         ),
+        cost_estimate=pl.CostEstimate(
+            flops=10**9, bytes_accessed=80 * 10**6, transcendentals=0
+        ),
         name="tail_exchange",
-    )(feat_in, user_in, both_in)
+    )(scale_in, user_in, both_in)
+
+
+def exchange(blocks, axes):
+    return lax.all_to_all(blocks, axes, split_axis=0, concat_axis=0, tiled=True)
 
 
 def local(
@@ -313,15 +317,18 @@
     n_columns = n_user * n_item
     sent = jnp.concatenate([side_matrix, feat_factor], axis=0)
     got = lax.all_to_all(sent, ("user", "item"), split_axis=1, concat_axis=0, tiled=True)
+    all_users = gather_rows(user_factor, "user")
+
+    user_sum, item_sum, week_sum = tile_sums(
+        tensor_tiles, tile_coords, tile_live, user_factor, item_factor, week_factor
+    )
+
+    got, user_sum, item_sum, week_sum = lax.optimization_barrier(
+        (got, user_sum, item_sum, week_sum)
+    )
     got = got.reshape(n_columns, sent.shape[0], got.shape[1])
     side_cols = got[:, :side_rows].reshape(n_columns * side_rows, got.shape[2])
     factor_cols = got[:, side_rows:].reshape(rank, got.shape[2])
-    all_users = gather_rows(user_factor, "user")
-
-    user_sum, item_sum, week_sum = tile_sums(
-        tensor_tiles, tile_coords, tile_live, user_factor, item_factor, week_factor
-    )
-
     both = jnp.concatenate([item_sum, week_sum], axis=0).T
     both = both.reshape(n_user, n_item, n_feat, own, item_rows + week_rows)
     both = both.transpose(0, 2, 1, 3, 4).reshape(
@@ -333,7 +340,11 @@
     feat_cols = lax.dot_general(
         all_users, side_resid, (((0,), (0,)), ((), ())), preferred_element_type=jnp.float32
     )
-    feat_cols = feat_cols.reshape(n_columns, rank // n_columns, feat_cols.shape[1])
+    width = feat_cols.shape[1]
+    scale = jnp.maximum(jnp.max(jnp.abs(feat_cols)), 1e-30) / 16384.0
+    own_ranks = rank // n_columns
+    coded = (feat_cols * (1.0 / scale)).astype(jnp.float16)
+    coded = exchange(coded.reshape(n_columns, own_ranks, width), ("user", "item"))
     side_user = lax.dot_general(
         side_resid, factor_cols, (((1,), (1,)), ((), ())), preferred_element_type=jnp.float32
     )
@@ -341,9 +352,16 @@
     user_total = lax.dynamic_update_slice_in_dim(side_user, mine + user_sum, user_base, 0)
     rows = user_total.shape[0] // (n_user * n_item * n_feat)
     by_feat = user_total.reshape(n_user * n_item, n_feat, rows, rank).transpose(1, 0, 2, 3)
-    grad_feat, grad_user, by_item, by_week = tail(feat_cols, by_feat, both, item_rows)
+    scales, grad_user, by_item, by_week = tail(
+        jnp.full((8, 128), scale), by_feat, both, item_rows
+    )
     grad_item = by_item.transpose(0, 2, 1).reshape(n_item * item_rows, own)
     grad_week = by_week.T
+    grad_feat = (
+        (coded.astype(jnp.float32) * scales[:, :1, :1])
+        .transpose(1, 0, 2)
+        .reshape(own_ranks, n_columns * width)
+    )
     return (grad_user, grad_item, grad_week, grad_feat)
 
 

time: 140 us -> 148 us (1.057)
  Pallas kernels: 54.8 us -> 47.8 us
  waiting for transfers between devices: 55.2 us -> 60.3 us
  matrix products: 3.51 us -> 7.65 us
  starting transfers between devices: 7.96 us -> 11.5 us
  other arithmetic: 2.49 us -> 4.9 us
    pallas_call x1, Pallas kernels: 51.8 us -> 44.8 us  [tail(): pl.pallas_call(tail_kernel, in_specs=[vmem] * 3, out_specs=[vmem] * 4, ou...]
    ppermute x1, waiting for transfers between devices: 16.5 us -> 20.5 us  [gather_rows(): lax.ppermute(block, axis, [(k, (k + shift) % count) for k in range(count)])]
    all_to_all x0 -> x1, starting transfers between devices: none -> 3.55 us  [exchange(): return lax.all_to_all(blocks, axes, split_axis=0, concat_axis=0, tiled=True)]
    dot_general x1, matrix products: 1 us -> 3.36 us  [local(): lax.dot_general(all_users, side_resid, (((0,), (0,)), ((), ())), preferre...]
    dot_general x1, matrix products: 1.27 us -> 3.03 us  [local(): lax.dot_general(side_resid, factor_cols, (((1,), (1,)), ((), ())), prefer...]
    unnamed x15 -> x20, local copies, waits for them, and re-layouts: 3.11 us -> 1.98 us
  transfers between devices with their start and end apart: 2 -> 3, of which waited for: 2 -> 2; matrix products, arithmetic and copies ran while one was open for 4% -> 7% of each run, Pallas kernels for 2% -> 33%
where the time goes in v4:
time: 148 us; the launch traced here: 147 us
  waiting for transfers between devices  60.3 us (41%)
  Pallas kernels  47.8 us (32%)
  local copies, waits for them, and re-layouts  13.1 us (9%)
  starting transfers between devices  11.5 us (8%)
  matrix products  7.65 us (5%)
  other arithmetic  4.9 us (3%)
  between operations  1.54 us (1%)
    pallas_call x1, Pallas kernels, tail(): pl.pallas_call(tail_kernel, in_specs=[vmem] * 3, out_specs=[vmem] * 4, ou...  44.8 us
    all_to_all x1, waiting for transfers between devices, local(): lax.all_to_all(sent, ('user', 'item'), split_axis=1, concat_axis=0, tiled...  39.8 us
    ppermute x1, waiting for transfers between devices, gather_rows(): lax.ppermute(block, axis, [(k, (k + shift) % count) for k in range(count)])  20.5 us
    all_to_all x1, starting transfers between devices, local(): lax.all_to_all(sent, ('user', 'item'), split_axis=1, concat_axis=0, tiled...  6.5 us
    all_to_all x1, starting transfers between devices, exchange(): return lax.all_to_all(blocks, axes, split_axis=0, concat_axis=0, tiled=True)  3.55 us
    dot_general x1, matrix products, local(): lax.dot_general(all_users, side_resid, (((0,), (0,)), ((), ())), preferre...  3.36 us
    dot_general x1, matrix products, local(): lax.dot_general(side_resid, factor_cols, (((1,), (1,)), ((), ())), prefer...  3.03 us
    pallas_call x1, Pallas kernels, tile_sums(): pl.pallas_call(tile_kernel, grid_spec=pltpu.PrefetchScalarGridSpec(num_sc...  2.98 us
  transfers between devices with their start and end apart: 3, of which 2 were waited for; matrix products, arithmetic and copies ran while one was open for 7% of the time, Pallas kernels for 33%

profile of v4, /device:TPU:1, one launch (start us, length us, event | category | flops | bytes accessed | tf_op | source)
XLA Modules:
  0.0 146.8 jit_solution(10861973126410014827)
XLA Ops:
  0.6 2.1 %pad_maximum_fusion = bf16[176,8192]{1,0:T(8,128)(2,1)S(1)} fusion(bf16[48,8192]{1,0:T(8,128)(2,1)} %param.15, bf16[128,8192]{1,0:T(8,128)(2,1)} %param.11), kind=kLoop, calls=%fused_computation.4 | loop fusion | flops 5767168 | bytes 5767168 | tf_op jit(solution)/shard_map/concatenate | solution.py:318
  2.8 1.9 %copy.37 = bf16[22,8,8,1024]{3,2,0,1:T(8,128)(2,1)} copy(bf16[22,8,8,1024]{3,2,1,0:T(8,128)(2,1)S(1)} %bitcast.44) | data formatting | bytes 5767168 | tf_op jit(solution)/shard_map/all_to_all | solution.py:319
  4.7 6.5 %all-to-all-start = ((bf16[176,8,1024]{2,0,1:T(8,128)(2,1)}), bf16[176,8,1024]{2,0,1:T(8,128)(2,1)}, u32[]{:S(2)}, u32[]{:S(2)}) async-start(bf16[176,8,1024]{2,0,1:T(8,128)(2,1)} %bitcast.43), calls=%async_computation | async-start | bytes 5767168 | tf_op jit(solution)/shard_map/all_to_all | solution.py:319
  11.2 1.5 collective-permute-start
  12.7 0.1 compare_select_fusion.2
  12.7 0.1 pad_add_fusion.starts
  12.8 3.0 %tile_sums.1 = (f32[512,384]{1,0:T(8,128)S(1)}, f32[512,384]{1,0:T(8,128)S(1)}, f32[256,384]{1,0:T(8,128)S(1)}) custom-call(s32[2,3]{1,0:T(2,128)S(1)} %pad_add_fusion.starts, s32[2]{0:T(128)S(1)} %copy-done.3, bf16[2,256,16384]{2,1,0:T(8,128)(2,1)} %tile.1, bf16[512,384]{1,0:T(8,128)(2,1)S(1)} %copy-done, bf16[512,384]{1,0:T(8,128)(2,1)S(1)} %copy-done.1, ...), custom_call_target="tpu_custom_call" | custom-call | flops 19327352832 | bytes 16777216 | tf_op jit(solution)/shard_map/tile_sums/pallas_call | solution.py:86
  15.8 0.1 broadcast_in_dim.6
  15.9 0.1 constant_dynamic-update-slice_fusion.1
  16.0 20.5 %collective-permute-done = bf16[512,384]{1,0:T(8,128)(2,1)S(1)} collective-permute-done((bf16[512,384]{1,0:T(8,128)(2,1)S(1)}, bf16[512,384]{1,0:T(8,128)(2,1)S(1)}, u32[]{:S(2)}, u32[]{:S(2)}) %collective-permute-start) | collective-permute-done | bytes 393248 | tf_op jit(solution)/shard_map/ppermute | solution.py:121
  36.6 39.8 %all-to-all-done = bf16[176,8,1024]{2,0,1:T(8,128)(2,1)} async-done(((bf16[176,8,1024]{2,0,1:T(8,128)(2,1)}), bf16[176,8,1024]{2,0,1:T(8,128)(2,1)}, u32[]{:S(2)}, u32[]{:S(2)}) %all-to-all-start) | async-done | bytes 2883616 | tf_op jit(solution)/shard_map/all_to_all | solution.py:319
  76.4 1.8 %slice.25 = bf16[8,128,1024]{2,1,0:T(8,128)(2,1)S(1)} slice(bf16[8,176,1024]{2,1,0:T(8,128)(2,1)} %bitcast.2), slice={[0:8], [0:128], [0:1024]} | slice | bytes 4194304 | tf_op jit(solution)/shard_map/slice | solution.py:330
  78.1 1.2 slice.24
  79.4 1.3 fusion.1
  80.6 3.4 %abs_reduce_fusion = (f32[]{:T(128)}, f32[384,1024]{1,0:T(8,128)S(1)}) fusion(bf16[1024,384]{1,0:T(8,128)(2,1)} %copy-done.4, bf16[1024,1024]{1,0:T(8,128)(2,1)S(1)} %fusion.1), kind=kOutput, calls=%fused_computation.8 | convolution fusion | flops 806092800 | bytes 4456452 | tf_op jit(solution)/shard_map/dot_general | solution.py:340
  84.7 1.1 multiply_convert_fusion
  85.8 3.5 %all-to-all-start.1 = ((f16[8,48,1024]{2,1,0:T(8,128)(2,1)}), f16[8,48,1024]{2,1,0:T(8,128)(2,1)S(1)}, u32[]{:S(2)}, u32[]{:S(2)}) async-start(f16[8,48,1024]{2,1,0:T(8,128)(2,1)} %bitcast.47), calls=%async_computation.1 | async-start | bytes 1572864 | tf_op jit(solution)/shard_map/all_to_all | solution.py:294
  89.3 3.0 %fusion.4 = f32[1024,384]{1,0:T(8,128)S(1)} fusion(bf16[1024,1024]{1,0:T(8,128)(2,1)} %copy-done.5, bf16[384,1024]{1,0:T(8,128)(2,1)} %bitcast.51), kind=kOutput, calls=%fused_computation.23 | convolution fusion | flops 805306368 | bytes 4456448 | tf_op jit(solution)/shard_map/dot_general | solution.py:348
  92.4 0.1 add_dynamic-update-slice_fusion
  92.5 0.1 copy.38
  92.6 1.1 maximum_bitcast_fusion
  93.7 1.6 %copy.27 = f32[384,768]{1,0:T(8,128)S(1)} copy(f32[384,768]{0,1:T(8,128)} %maximum_bitcast_fusion) | data formatting | bytes 2359296 | tf_op jit(solution)/shard_map/transpose | solution.py:332
  95.4 1.3 reshape.41
  96.6 1.5 %copy.28 = f32[2,4,4,12,768]{4,3,2,1,0:T(8,128)S(1)} copy(f32[2,4,4,12,768]{4,3,1,2,0:T(8,128)} %bitcast.45) | data formatting | bytes 2359296 | tf_op jit(solution)/shard_map/transpose | solution.py:334
  98.2 44.8 %tail_exchange.1 = (f32[8,8,128]{2,1,0:T(8,128)S(1)}, f32[32,384]{1,0:T(8,128)S(1)}, f32[4,12,512]{2,1,0:T(8,128)S(1)}, f32[12,256]{1,0:T(8,128)S(1)}) custom-call(f32[8,128]{1,0:T(8,128)S(1)} %broadcast_in_dim.7.scale_in, f32[4,8,32,384]{3,2,1,0:T(8,128)S(1)} %bitcast.39, f32[8,4,12,768]{3,2,1,0:T(8,128)S(1)} %bitcast.40), custom_call_target="tpu_custom_call" | custom-call | flops 1000000000 | bytes 80000000 | tf_op jit(solution)/shard_map/tail_exchange/pallas_call | solution.py:259
  143.0 0.1 copy.39
  143.1 0.7 copy.33
  143.8 0.1 slice_reduce_fusion
  144.0 0.3 multiply_bitcast_fusion
  144.3 1.3 copy.32
  145.5 0.6 copy.45
  146.1 0.6 copy.46
  (20 shorter events, 0.1 us)
Async XLA Ops:
  4.7 6.5 %copy-start = (bf16[512,384]{1,0:T(8,128)(2,1)S(1)}, bf16[512,384]{1,0:T(8,128)(2,1)}, u32[]{:S(2)}) copy-start(bf16[512,384]{1,0:T(8,128)(2,1)} %user.1) | copy-start | bytes 1179652
  4.7 8.0 %copy-start.7 = (s32[2,3]{1,0:T(2,128)S(1)}, s32[2,3]{1,0:T(2,128)}, u32[]{:S(2)}) copy-start(s32[2,3]{1,0:T(2,128)} %param.9) | copy-start | bytes 76
  4.7 8.1 %copy-start.1 = (bf16[512,384]{1,0:T(8,128)(2,1)S(1)}, bf16[512,384]{1,0:T(8,128)(2,1)}, u32[]{:S(2)}) copy-start(bf16[512,384]{1,0:T(8,128)(2,1)} %item.1) | copy-start | bytes 1179652
  4.7 8.1 %copy-start.2 = (bf16[256,384]{1,0:T(8,128)(2,1)S(1)}, bf16[256,384]{1,0:T(8,128)(2,1)}, u32[]{:S(2)}) copy-start(bf16[256,384]{1,0:T(8,128)(2,1)} %week.1) | copy-start | bytes 589828
  4.7 8.1 %copy-start.3 = (s32[2]{0:T(128)S(1)}, s32[2]{0:T(128)}, u32[]{:S(2)}) copy-start(s32[2]{0:T(128)} %live.1) | copy-start | bytes 28
  4.7 71.7 %all-to-all-start = ((bf16[176,8,1024]{2,0,1:T(8,128)(2,1)}), bf16[176,8,1024]{2,0,1:T(8,128)(2,1)}, u32[]{:S(2)}, u32[]{:S(2)}) async-start(bf16[176,8,1024]{2,0,1:T(8,128)(2,1)} %bitcast.43), calls=%async_computation | async-start | bytes 5767168 | tf_op jit(solution)/shard_map/all_to_all | solution.py:319
  11.2 25.3 %collective-permute-start = (bf16[512,384]{1,0:T(8,128)(2,1)S(1)}, bf16[512,384]{1,0:T(8,128)(2,1)S(1)}, u32[]{:S(2)}, u32[]{:S(2)}) collective-permute-start(bf16[512,384]{1,0:T(8,128)(2,1)S(1)} %copy-done), channel_id=1, source_target_pairs={{0,16},{16,0},{1,17},{17,1},{2,18},{18,2},{3,19},{19,3},{4,20},{20... | collective-permute-start | bytes 1179656 | tf_op jit(solution)/shard_map/ppermute | solution.py:121
  36.6 42.8 %copy-start.4 = (bf16[1024,384]{1,0:T(8,128)(2,1)}, bf16[1024,384]{1,0:T(8,128)(2,1)S(1)}, u32[]{:S(2)}) copy-start(bf16[1024,384]{1,0:T(8,128)(2,1)S(1)} %constant_dynamic-update-slice_fusion) | copy-start | bytes 2359300
  79.3 1.3 copy-start.6
  80.6 3.4 %copy-start.5 = (bf16[1024,1024]{1,0:T(8,128)(2,1)}, bf16[1024,1024]{1,0:T(8,128)(2,1)S(1)}, u32[]{:S(2)}) copy-start(bf16[1024,1024]{1,0:T(8,128)(2,1)S(1)} %fusion.1) | copy-start | bytes 6291460
  85.8 58.2 %all-to-all-start.1 = ((f16[8,48,1024]{2,1,0:T(8,128)(2,1)}), f16[8,48,1024]{2,1,0:T(8,128)(2,1)S(1)}, u32[]{:S(2)}, u32[]{:S(2)}) async-start(f16[8,48,1024]{2,1,0:T(8,128)(2,1)} %bitcast.47), calls=%async_computation.1 | async-start | bytes 1572864 | tf_op jit(solution)/shard_map/all_to_all | solution.py:294
